TPU v7x, 32 devices: a whole 2x2x4 slice. The times are simulated.
32 devices in a mesh: dp: 8 (over z, y), fsdp: 4 (over x, core).
Axes of the slice: x: 2, y: 2, z: 4, core: 2. Of those that a mesh axis runs over, the one named last changes fastest.
Arguments:
- inputs: bfloat16 [32768, 768], P(('dp', 'fsdp')), may hold values from -6 to 6
- lengths: int32 [64, 2], P(('dp', 'fsdp')), may hold values from 1 to 507, as said below
- query_matrix: bfloat16 [768, 768], P(('dp', 'fsdp')), may hold values from -0.21875 to 0.21875
- key_weight: bfloat16 [768, 768], P(('dp', 'fsdp')), may hold values from -0.21875 to 0.21875
- value_matrix: bfloat16 [768, 768], P(('dp', 'fsdp')), may hold values from -0.21875 to 0.21875
- output_weight: bfloat16 [768, 768], P(('dp', 'fsdp')), may hold values from -1.25 to 1.25
- inner_weight: bfloat16 [768, 3072], P(('dp', 'fsdp')), may hold values from -0.21875 to 0.21875
- outer_weight: bfloat16 [3072, 768], P(('dp', 'fsdp')), may hold values from -0.109375 to 0.109375
- attn_gain: bfloat16 [768], replicated, may hold values from 0.5 to 1.5
- attn_shift: bfloat16 [768], replicated, may hold values from -1.5 to 1.5
- ffn_gain: bfloat16 [768], replicated, may hold values from 0.5 to 1.5
- ffn_shift: bfloat16 [768], replicated, may hold values from -1.5 to 1.5
- query_down: float32 [768, 8], replicated, may hold values from -0.21875 to 0.21875
- query_raise_weight: float32 [8, 768], replicated, may hold values from -1 to 1
- value_down: float32 [768, 8], replicated, may hold values from -0.21875 to 0.21875
- value_raise_weight: float32 [8, 768], replicated, may hold values from -1 to 1
- grad_output: bfloat16 [32768, 768], P(('dp', 'fsdp')), may hold values from -6 to 6
Outputs:
- outputs: bfloat16 [32768, 768], P(('dp', 'fsdp'))
- grad_inputs: float32 [32768, 768], P(('dp', 'fsdp'))
- grad_query_down: float32 [768, 8], replicated
- grad_query_up: float32 [8, 768], replicated
- grad_value_down: float32 [768, 8], replicated
- grad_value_up: float32 [8, 768], replicated
Inputs may be any that keep to these rules, and one draw needn't show every extreme that they name: lengths[s, 0] and lengths[s, 1] are slot s's premise and hypothesis token counts, each 1 or more, with lengths[s, 0] + lengths[s, 1] + 4 <= 512; in every draw some slot has lengths[s, 0] + lengths[s, 1] + 4 == 512.
All inputs are finite; a program needn't handle non-finite values.
Results may differ from a plain program's by a relative error of at most 0.017.
The roundings to bfloat16 on the way count: a program that leaves them out, or rounds other values in their place, can miss the bound.
Values may be sent and summed in bfloat16 or wider, within the bound.
No kernel may reach another device: no remote copies, remote signals or barrier semaphores. Data moves between devices by JAX's collectives and lax.ppermute only.
A program may use at most 128 MiB of HBM per device.

v0:
```python
import functools
import jax
import jax.numpy as jnp
from jax import lax
from jax.experimental import pallas as pl
from jax.experimental.pallas import tpu as pltpu
from jax.sharding import PartitionSpec as P

HEAD_DIM=64; SLOT=512
F32=jnp.float32; BF=jnp.bfloat16
MIB=1024*1024
AXES=("dp","fsdp")
sd=jax.ShapeDtypeStruct
ANY=pl.BlockSpec(memory_space=pl.ANY)
HELD=pl.BlockSpec(memory_space=pltpu.VMEM)
SCALARS=pl.BlockSpec(memory_space=pltpu.SMEM)


def params(mib=56):
    return pltpu.CompilerParams(vmem_limit_bytes=mib*MIB)

def takes(us):
    return pl.CostEstimate(flops=int(us*1.1e9),bytes_accessed=0,transcendentals=0)


def dg(a,b,ca,cb):
    return lax.dot_general(a,b,(((ca,),(cb,)),((),())),preferred_element_type=F32)

def far(v):
    return pltpu.with_memory_space_constraint(v,pltpu.HBM)


def block_copies(me,bufs,to,sems):
    if len(bufs)==1:
        return [pltpu.make_async_copy(bufs[0],to,sems.at[0])]
    chip=lax.div(me,2); core=lax.rem(me,2)
    copies=[]
    for which,buf in enumerate(bufs):
        origin=core if which<2 else 1-core
        _,_,rows,half=buf.shape
        for i in range(8):
            dst=lax.bitwise_xor(chip,(which%2)*(2-origin)+(i//4)*(1+origin)+4*(i%4))
            at=to.at[:,pl.ds(pl.multiple_of(dst*rows,16),rows),pl.ds(pl.multiple_of(origin*half,128),half)]
            copies.append(pltpu.make_async_copy(buf.at[i],at,sems.at[len(copies)]))
    return copies

def start_all(copies):
    for c in copies: c.start()

def wait_all(copies):
    for c in copies: c.wait()

BLOCK_COPIES=32

def prep_kernel(qdt_ref,vdt_ref,qu_ref,vu_ref,ag_ref,ash_ref,fg_ref,fsh_ref,dn_ref,upq_ref,upv_ref,dnt_ref,nm_ref):
    D=qu_ref.shape[1]
    both=jnp.concatenate([qdt_ref[...],vdt_ref[...]],axis=0)
    dnt_ref[...]=both.astype(BF)
    dn_ref[...]=jnp.concatenate([both,jnp.zeros((112,D),F32)],axis=0).T.astype(BF)
    z8=jnp.zeros((8,D),F32); z=jnp.zeros((112,D),F32)
    upq_ref[...]=jnp.concatenate([qu_ref[...],z8,z],axis=0).astype(BF)
    upv_ref[...]=jnp.concatenate([z8,vu_ref[...],z],axis=0).astype(BF)
    for i,r in enumerate((ag_ref,ash_ref,fg_ref,fsh_ref)):
        nm_ref[i:i+1,:]=r[...].astype(F32)
    nm_ref[4:8,:]=jnp.zeros((4,D),F32)

def prep(qd,qu,vd,vu,ag,ash,fg,fsh):
    D=qu.shape[1]
    return pl.pallas_call(prep_kernel,out_shape=[sd((D,128),BF),sd((128,D),BF),sd((128,D),BF),sd((16,D),BF),sd((8,D),F32)],
        compiler_params=params(8),cost_estimate=takes(1),name="prep")(qd.T,vd.T,qu,vu,*(v.reshape(1,D) for v in (ag,ash,fg,fsh)))


def low_kernel(x_ref,dn_ref,upq_ref,upv_ref,low_ref,lq_ref,lv_ref):
    for s in range(x_ref.shape[0]//SLOT):
        r=slice(s*SLOT,(s+1)*SLOT)
        low=dg(x_ref[r,:],dn_ref[...],1,0).astype(BF)
        low_ref[:,r]=low.T[:32]
        lq_ref[r,:]=2.0*dg(low,upq_ref[...],1,0)
        lv_ref[r,:]=2.0*dg(low,upv_ref[...],1,0)

def low_rank(x,dn,upq,upv):
    rows,D=x.shape
    return pl.pallas_call(low_kernel,in_specs=[HELD]*4,out_specs=[HELD]*3,
        out_shape=[sd((32,rows),BF),pltpu.VMEM((rows,D),F32),pltpu.VMEM((rows,D),F32)],
        compiler_params=params(LIM["low_rank"]),cost_estimate=takes(3),name="low_rank")(x,dn,upq,upv)

def project_kernel(sc_ref,x_ref,lq_ref,lv_ref,*rest):
    *blocks,qkv_ref,wo,w,sems,osem=rest
    i=pl.program_id(0); D=x_ref.shape[1]
    whole=[pltpu.make_async_copy(w,wo,osem.at[0])]
    @pl.when(i==0)
    def _():
        copies=block_copies(sc_ref[0],blocks,w,sems)
        start_all(copies); wait_all(copies); start_all(whole)
    r=pl.ds(pl.multiple_of(i*SLOT,SLOT),SLOT)
    for t,up in enumerate((lq_ref,None,lv_ref)):
        v=dg(x_ref[r,:],w[t],1,0)
        if up is not None: v=v+up[r,:]
        qkv_ref[r,t*D:(t+1)*D]=v.astype(BF)
    @pl.when(i==pl.num_programs(0)-1)
    def _(): wait_all(whole)

def project(scalars,x,lq,lv,blocks):
    rows,D=x.shape
    return pl.pallas_call(project_kernel,grid=(rows//SLOT,),
        in_specs=[SCALARS,HELD,HELD,HELD]+[ANY]*len(blocks),
        out_specs=[HELD,ANY],
        out_shape=[pltpu.VMEM((rows,3*D),BF),pltpu.HBM((3,D,D),BF)],
        scratch_shapes=[pltpu.VMEM((3,D,D),BF),pltpu.SemaphoreType.DMA((BLOCK_COPIES,)),pltpu.SemaphoreType.DMA((1,))],
        compiler_params=params(LIM["project"]),cost_estimate=takes(8),name="project")(scalars,x,lq,lv,*blocks)

def attend_kernel(sc_ref,qkv_ref,e_ref,ot_ref,o_ref,rt_ref):
    s=pl.program_id(0); j=pl.program_id(1); J=pl.num_programs(1); D=256*J
    lane=lax.broadcasted_iota(jnp.int32,(SLOT,128),1)
    row=lax.broadcasted_iota(jnp.int32,(SLOT,128),0)
    bias=jnp.where(row<sc_ref[1+s],0.0,-1e30).astype(F32)
    rows=pl.ds(pl.multiple_of(s*SLOT,SLOT),SLOT)
    def part(which,p):
        return qkv_ref[rows,pl.ds(pl.multiple_of(which*D+256*j+128*p,128),128)].astype(F32)
    heads=[]
    for p in range(2):
        qp,kp,vp=part(0,p)*0.125,part(1,p),part(2,p)
        for h in range(2):
            own=(lane<64) if h==0 else (lane>=64)
            aux=64 if h==0 else 0
            one=jnp.where(lane==aux,1.0,0.0)
            heads.append((64*h,aux,jnp.where(own,qp,one).astype(BF),
                          jnp.where(own,kp,jnp.where(lane==aux,bias,0.0)).astype(BF),jnp.where(own,vp,one).astype(BF)))
    totals=[]; os=[]
    def weights(n,st):
        e_ref[n]=jnp.exp(st-jnp.max(st,axis=0,keepdims=True)).astype(BF)
    def mix(n):
        lo,aux,_,_,vm=heads[n]
        ot=dg(vm,e_ref[n],0,0)
        r=1.0/ot[aux:aux+1]
        totals.append(r)
        os.append((ot[lo:lo+64]*r).astype(BF))
    before=None
    for n in range(4):
        st=dg(heads[n][3],heads[n][2],1,1)
        if before is not None:
            weights(n-1,before)
            if n>1: mix(n-2)
        before=st
    weights(3,before)
    mix(2); mix(3)
    ot=jnp.concatenate(os,axis=0)
    ot_ref[...]=ot
    o_ref[rows,pl.ds(pl.multiple_of(256*j,256),256)]=ot.T
    rt_ref[0]=jnp.concatenate(totals+totals,axis=0)

def attend(scalars,qkv,slots):
    rows=qkv.shape[0]; D=qkv.shape[1]//3; J=D//256; H=D//HEAD_DIM
    return pl.pallas_call(attend_kernel,grid=(slots,J),
        in_specs=[SCALARS,HELD],
        out_specs=[pl.BlockSpec((4,SLOT,SLOT),lambda s,j:(s*J+j,0,0)),pl.BlockSpec((256,SLOT),lambda s,j:(s*J+j,0)),HELD,pl.BlockSpec((1,8,SLOT),lambda s,j:(s*J+j,0,0))],
        out_shape=[pltpu.HBM((slots*H,SLOT,SLOT),BF),pltpu.HBM((slots*D,SLOT),BF),pltpu.VMEM((rows,D),BF),pltpu.HBM((slots*J,8,SLOT),F32)],
        compiler_params=params(LIM["attend"]),cost_estimate=takes(16),name="attend")(scalars,qkv)


def norm_stats(value):
    mean=jnp.mean(value,axis=-1,keepdims=True)
    c=value-mean
    r=lax.rsqrt(jnp.mean(c*c,axis=-1,keepdims=True)+1e-5)
    return c*r,r

def norm_back(g,n,r):
    return r*(g-jnp.mean(g,axis=-1,keepdims=True)-n*jnp.mean(g*n,axis=-1,keepdims=True))

def gelu_pair(v):
    cdf=0.5+0.5*lax.erf(v*0.7071067811865476)
    return v*cdf, cdf+(0.3989422804014327*v)*jnp.exp(-0.5*v*v)

CH=256
LIM={"project":10,"attend":12,"feed_in":8,"feed_out":18,"attend_back":12,"inputs_grad":10,"low_rank":10}

def feed_in_kernel(sc_ref,x_ref,o_ref,nm_ref,*rest):
    *blocks,n1_ref,r1_ref,act_ref,gp_ref,w,sems=rest
    i=pl.program_id(0); D=x_ref.shape[1]
    @pl.when(i==0)
    def _():
        copies=block_copies(sc_ref[0],blocks,w,sems)
        start_all(copies); wait_all(copies)
    rows=pl.ds(pl.multiple_of(i*SLOT,SLOT),SLOT)
    first=x_ref[rows,:].astype(F32)+dg(o_ref[rows,:],w[0],1,0)
    n1,r1=norm_stats(first)
    n1_ref[rows,:]=n1; r1_ref[rows,:]=jnp.broadcast_to(r1,(SLOT,128))
    hb=(n1*nm_ref[0:1,:]+nm_ref[1:2,:]).astype(BF)
    for c in range(0,act_ref.shape[1],CH):
        act,gp=gelu_pair(dg(hb,w[1+c//D,:,c%D:c%D+CH],1,0))
        act_ref[rows,c:c+CH]=act.astype(BF)
        gp_ref[rows,c:c+CH]=gp.astype(BF)

def feed_in(scalars,x,o,nm,blocks,FF):
    rows,D=x.shape
    return pl.pallas_call(feed_in_kernel,grid=(rows//SLOT,),
        in_specs=[SCALARS,HELD,HELD,HELD]+[ANY]*len(blocks),
        out_specs=[HELD]*5,
        out_shape=[pltpu.VMEM((rows,D),F32),pltpu.VMEM((rows,128),F32),pltpu.VMEM((rows,FF),BF),pltpu.VMEM((rows,FF),BF),pltpu.VMEM((1+FF//D,D,D),BF)],
        scratch_shapes=[pltpu.SemaphoreType.DMA((BLOCK_COPIES,))],
        compiler_params=params(LIM["feed_in"]),cost_estimate=takes(14),name="feed_in")(scalars,x,o,nm,*blocks)

def feed_out_kernel(sc_ref,n1_ref,r1_ref,act_ref,gp_ref,go_ref,nm_ref,w,*rest):
    *blocks,out_ref,gfs_ref,gmt_ref,gi_ref,wt,sems=rest
    copies=block_copies(sc_ref[0],blocks,wt,sems)
    start_all(copies); wait_all(copies)
    rows,D=go_ref.shape; FF=gi_ref.shape[1]
    ag,ash,fg,fsh=(nm_ref[i:i+1,:] for i in range(4))
    part=[slice(s*SLOT,(s+1)*SLOT) for s in range(rows//SLOT)]
    acc={}; g2={}; g1={}
    def second_sum(s):
        acc[s]=n1_ref[part[s],:]*ag+ash+dg(act_ref[part[s],:],wt[0],1,0)
    def second_norm(s):
        n2,r2=norm_stats(acc[s])
        out_ref[part[s],:]=(n2*fg+fsh).astype(BF)
        g2[s]=norm_back(go_ref[part[s],:].astype(F32)*fg,n2,r2)
    def inner_grad(s):
        g=g2[s].astype(BF)
        for c in range(0,FF,CH):
            ga=dg(g,wt[0,c:c+CH,:],1,1)
            gi_ref[part[s],c:c+CH]=(ga*gp_ref[part[s],c:c+CH].astype(F32)).astype(BF)
    def first_grad(s):
        v=g2[s]
        for b in range(FF//D): v=v+dg(gi_ref[part[s],b*D:(b+1)*D],w[1+b],1,1)
        acc[s]=v
    def first_norm(s):
        g=norm_back(acc[s]*ag,n1_ref[part[s],:],r1_ref[part[s],0:1])
        gfs_ref[part[s],:]=g
        g1[s]=g.astype(BF)
    def mixed_grad(s):
        gmt_ref[:,part[s]]=dg(w[0],g1[s],1,1).astype(BF)
    stages=(second_sum,second_norm,inner_grad,first_grad,first_norm,mixed_grad)
    order=sorted((2*k+(3*s if k else 0),s,k) for s in range(len(part)) for k in range(len(stages)))
    for _,s,k in order:
        stages[k](s)

def feed_out(scalars,n1,r1,act,gp,go,w,nm,blocks):
    rows,D=n1.shape; FF=act.shape[1]
    return pl.pallas_call(feed_out_kernel,
        in_specs=[SCALARS]+[HELD]*7+[ANY]*len(blocks),
        out_specs=[HELD]*4,
        out_shape=[sd((rows,D),BF),pltpu.VMEM((rows,D),F32),pltpu.VMEM((D,rows),BF),pltpu.VMEM((rows,FF),BF)],
        input_output_aliases={3:3},
        scratch_shapes=[pltpu.VMEM((1,FF,D),BF),pltpu.SemaphoreType.DMA((BLOCK_COPIES,))],
        compiler_params=params(LIM["feed_out"]),cost_estimate=takes(24),name="feed_out")(scalars,n1,r1,act,gp,go,nm,w,*blocks)[:3]


def attend_back_kernel(sc_ref,q_ref,k_ref,v_ref,e_ref,ot_ref,rt_ref,gmt_ref,x_ref,low_ref,upq_ref,upv_ref,
                       d_ref,gl_ref,mine_ref,other_ref,glacc,ad_ref):
    s=pl.program_id(0); j=pl.program_id(1); J=pl.num_programs(1)
    lane=lax.broadcasted_iota(jnp.int32,(SLOT,128),1)
    rowi=lax.broadcasted_iota(jnp.int32,(128,SLOT),0)
    D=256*J
    rows=pl.ds(pl.multiple_of(s*SLOT,SLOT),SLOT)
    def place_of(which,p):
        return rows,pl.ds(pl.multiple_of(which*D+256*j+128*p,128),128)
    gmq=gmt_ref[pl.ds(pl.multiple_of(256*j,256),256),rows]
    otq=ot_ref[...]
    dqts=[]; dvs=[]
    for p in range(2):
        cols=slice(128*p,128*p+128)
        qp,kp,vp=(w[:,cols].astype(F32) for w in (q_ref,k_ref,v_ref))
        qp=qp*0.125; kp=kp*0.125
        gm=gmq[cols,:].astype(F32); om=otq[cols,:].astype(F32)
        pr=gm*om
        dkp=None; dvp=None; dqt=None
        for h in range(2):
            own=(lane<64) if h==0 else (lane>=64)
            ownr=(rowi<64) if h==0 else (rowi>=64)
            aux=64 if h==0 else 0
            r=rt_ref[0,2*p+h:2*p+h+1,:]
            d=-jnp.sum(pr[64*h:64*h+64],axis=0,keepdims=True)*r
            dhi=d.astype(BF).astype(F32)
            dlo=d-dhi
            gs=gm*r
            gaug=jnp.where(ownr,gs,jnp.where(rowi==aux,dhi,jnp.where(rowi==aux+1,dlo,0.0))).astype(BF)
            gown=jnp.where(ownr,gs,0.0).astype(BF)
            vm=jnp.where(own,vp,jnp.where((lane==aux)|(lane==aux+1),1.0,0.0)).astype(BF)
            e=e_ref[2*p+h]
            ds=(dg(vm,gaug,1,0)*e.astype(F32)).astype(BF)
            qm=jnp.where(own,qp,0.0).astype(BF)
            km=jnp.where(own,kp,0.0).astype(BF)
            dv=dg(e,gown,1,1)
            dk=dg(ds,qm,1,0)
            dq=dg(km,ds,0,0)
            dvp=dv if dvp is None else dvp+dv
            dkp=dk if dkp is None else dkp+dk
            dqt=dq if dqt is None else dqt+dq
        d_ref[place_of(1,p)]=dkp.astype(BF)
        dvs.append(dvp.astype(BF))
        d_ref[place_of(2,p)]=dvs[p]
        dqts.append(dqt.astype(BF))
    dqt=jnp.concatenate(dqts,axis=0)
    dqb=dqt.T
    d_ref[rows,pl.ds(pl.multiple_of(256*j,256),256)]=dqb
    dvb=jnp.concatenate(dvs,axis=1)
    glq=dg(upq_ref[...],dqt,1,0)
    glv=dg(upv_ref[...],dvb,1,1)
    part=2.0*(glq+glv)
    @pl.when(j==0)
    def _(): glacc[...]=part
    @pl.when(j>0)
    def _(): glacc[...]+=part
    low=low_ref[...]
    c0=pl.multiple_of(j*256,256)
    upq=2.0*dg(low[:16],dqb,1,0)
    upv=2.0*dg(low[:16],dvb,1,0)
    upg=jnp.concatenate([upq[0:8],upv[8:16]],axis=0)
    def add(rows,cols,v):
        @pl.when(s==0)
        def _(): ad_ref[rows,cols]=v
        @pl.when(s>0)
        def _(): ad_ref[rows,cols]+=v
    add(slice(16,32),pl.ds(c0,256),upg)
    @pl.when(j==J-1)
    def _():
        gl=glacc[...].astype(BF)
        gl_ref[...]=gl
        add(slice(0,16),slice(None),dg(gl,x_ref[...],1,0))
        core=lax.rem(sc_ref[0],2)
        for c,(a,b) in enumerate(((mine_ref,other_ref),(other_ref,mine_ref))):
            @pl.when((s==pl.num_programs(0)-1)&(core==c))
            def _():
                a[...]=ad_ref[0:16,:]
                b[...]=ad_ref[16:32,:]

def attend_back(scalars,qkv,e,ot,rt,gmt,x,low,upq,upv):
    rows,D=x.shape; J=D//256; S=rows//SLOT
    up=pl.BlockSpec((16,256),lambda s,j:(0,j))
    return pl.pallas_call(attend_back_kernel,grid=(S,J),
        in_specs=[SCALARS,*[pl.BlockSpec((SLOT,256),lambda s,j,w=w:(s,w*J+j)) for w in range(3)],
                  pl.BlockSpec((4,SLOT,SLOT),lambda s,j:(s*J+j,0,0)),pl.BlockSpec((256,SLOT),lambda s,j:(s*J+j,0)),
                  pl.BlockSpec((1,8,SLOT),lambda s,j:(s*J+j,0,0)),HELD,
                  pl.BlockSpec((SLOT,D),lambda s,j:(s,0)),pl.BlockSpec((32,SLOT),lambda s,j:(0,s)),up,up],
        out_specs=[HELD,pl.BlockSpec((16,SLOT),lambda s,j:(0,s)),HELD,HELD],
        out_shape=[pltpu.VMEM((rows,3*D),BF),sd((16,rows),BF),pltpu.VMEM((16,D),F32),pltpu.VMEM((16,D),F32)],
        scratch_shapes=[pltpu.VMEM((16,SLOT),F32),pltpu.VMEM((32,D),F32)],
        compiler_params=params(LIM["attend_back"]),cost_estimate=takes(18),name="attend_back")(scalars,far(qkv),far(qkv),far(qkv),far(e),far(ot),rt,gmt,x,low,upq,upv)

def inputs_kernel(gfs_ref,d_ref,gl,w_ref,dnt_ref,out_ref):
    T=gfs_ref.shape[0]
    rows=pl.ds(pl.multiple_of(pl.program_id(0)*T,T),T)
    D=gfs_ref.shape[1]
    v=gfs_ref[...]+dg(gl[...],dnt_ref[...],0,0)
    for t in range(3): v=v+dg(d_ref[rows,t*D:(t+1)*D],w_ref[t],1,1)
    out_ref[...]=v

def inputs_grad(gfs,d,gl,w,dnt):
    rows,D=gfs.shape
    row=pl.BlockSpec((SLOT,D),lambda i:(i,0))
    return pl.pallas_call(inputs_kernel,grid=(rows//SLOT,),
        in_specs=[row,HELD,pl.BlockSpec((16,SLOT),lambda i:(0,i)),HELD,HELD],
        out_specs=row,out_shape=sd((rows,D),F32),
        compiler_params=params(LIM["inputs_grad"]),cost_estimate=takes(7),name="inputs_grad")(gfs,d,gl,w,dnt)


def device_count():
    return lax.axis_size("dp")*lax.axis_size("fsdp")

def permute(v,target):
    return lax.ppermute(v,AXES,[(i,target(i)) for i in range(device_count())])

def exchange(v,mask):
    return permute(v,lambda i:i^mask)

def along_z(block):
    top=device_count()//4
    return [block]+[exchange(block,top*m) for m in (1,2,3)]

def near_hop(v):
    return permute(v,lambda i:i^(4 if i%2 else 2))

def far_hop(v):
    return permute(v,lambda i:i^(2 if i%2 else 4))

def in_bands(bands,*blocks):
    return tuple(b.reshape(8,bands,-1,b.shape[2]) for b in blocks)

def core_pair(v):
    groups=[[2*i,2*i+1] for i in range(lax.axis_size("fsdp")//2)]
    return lax.all_gather(v,"fsdp",axis=0,tiled=False,axis_index_groups=groups)

def column_half(both):
    c=lax.axis_index("fsdp")%2
    half=both.shape[2]//2
    return lax.dynamic_slice_in_dim(both,c*half,half,axis=2).reshape(-1,half)

def total_over_devices(mine,other,meanwhile):
    n=device_count()
    mine=mine+exchange(other,1)
    got=[exchange(mine,m) for m in range(2,n//4,2)]
    for g in got: mine=mine+g
    got=[exchange(mine,m) for m in (n//4,n//2,3*n//4)]
    got,done=tie(got,meanwhile())
    for g in got: mine=mine+g
    return mine,exchange(mine,1),done

def finish_kernel(scale,sc_ref,mine_ref,other_ref,*outs):
    core=lax.rem(sc_ref[0],2)
    for c,halves in enumerate(((mine_ref,other_ref),(other_ref,mine_ref))):
        @pl.when(core==c)
        def _():
            for i,o in enumerate(outs): o[...]=halves[i//2][8*(i%2):8*(i%2)+8,:]*scale

def finish(scalars,mine,other,scale):
    D=mine.shape[1]
    return pl.pallas_call(functools.partial(finish_kernel,scale),in_specs=[SCALARS,HELD,HELD],out_specs=[HELD]*4,
        out_shape=[sd((8,D),F32)]*4,compiler_params=params(8),cost_estimate=takes(1),name="finish")(scalars,mine,other)

def tie(*v):
    return lax.optimization_barrier(v)

def by_hops(scalars,x,wq,wk,wv,wo,wi,wt,ag,ash,fg,fsh,qd,qu,vd,vu,go):
    D=wq.shape[1]; FF=wi.shape[1]; bands=FF//D; r=wq.shape[0]
    top=device_count()//4
    both=core_pair(jnp.concatenate([wq,wk,wv],0))
    s1=jnp.concatenate([column_half(both[:,r*t:r*t+r]) for t in range(3)],0)
    z1=along_z(s1)
    wo,wi,wt,qd,s1=tie(wo,wi,wt,qd,s1)
    bo,bi,bt=core_pair(wo),core_pair(wi),core_pair(wt)
    s2=jnp.concatenate([column_half(bo)]+[column_half(bi[:,:,D*t:D*t+D]) for t in range(bands)],0)
    s3=column_half(bt)
    dn,upq,upv,dnt,nm=prep(qd,qu,vd,vu,ag,ash,fg,fsh)
    n3=near_hop(s3)
    z1,s2,dn,scalars=tie(z1,s2,dn,scalars)
    a1=jnp.stack(z1,0)
    n1=near_hop(a1)
    z2=exchange(s2,2*top)
    b3=jnp.stack([s3,n3],0)
    y3=exchange(b3,top)
    n1,z2,s2,n3,dn=tie(n1,z2,s2,n3,dn)
    f1=jnp.concatenate([a1,n1],0)
    h1=far_hop(f1); of1=exchange(f1,1)
    e2=jnp.stack([s2,z2],0)
    y2=exchange(e2,top)
    m2=near_hop(e2)
    low,lq,lv=low_rank(x,dn,upq,upv)
    y2,y3,lq=tie(y2,y3,lq)
    n2=near_hop(y2)
    g3=jnp.stack([b3,y3],0)
    z3=exchange(g3,2*top)
    h1,of1=tie(h1,of1)
    oh1=exchange(h1,1)
    oh1,=tie(oh1)
    f2=jnp.stack([e2[0],y2[0],e2[1],y2[1],m2[0],n2[0],m2[1],n2[1]],0)
    h2=far_hop(f2); of2=exchange(f2,1)
    qkv,wqkv=project(scalars,x,lq,lv,in_bands(3,f1,h1,of1,oh1))
    e,ot,o,rt=attend(scalars,qkv,x.shape[0]//SLOT)
    h2,o,of2,z3=tie(h2,o,of2,z3)
    oh2=exchange(h2,1)
    f3=jnp.concatenate([g3,z3],0).swapaxes(0,1).reshape(8,-1,D//2)
    h3=far_hop(f3); of3=exchange(f3,1)
    oh2,=tie(oh2)
    nn,r1,act,gp,w=feed_in(scalars,x,o,nm,in_bands(1+bands,f2,h2,of2,oh2),FF)
    h3,nn,of3=tie(h3,nn,of3)
    oh3=exchange(h3,1)
    out,gfs,gmt=feed_out(scalars,nn,r1,act,gp,go,w,nm,in_bands(1,f3,h3,of3,oh3))
    return qkv,low,wqkv,e,ot,rt,out,gfs,gmt,upq,upv,dnt

def by_all_gather(scalars,x,wq,wk,wv,wo,wi,wt,ag,ash,fg,fsh,qd,qu,vd,vu,go):
    wq,wk,wv,wo,wi,wt=(lax.all_gather(w,AXES,axis=0,tiled=True) for w in (wq,wk,wv,wo,wi,wt))
    D=wq.shape[1]; FF=wi.shape[1]
    dn,upq,upv,dnt,nm=prep(qd,qu,vd,vu,ag,ash,fg,fsh)
    low,lq,lv=low_rank(x,dn,upq,upv)
    qkv,wqkv=project(scalars,x,lq,lv,(jnp.stack([wq,wk,wv],0),))
    e,ot,o,rt=attend(scalars,qkv,x.shape[0]//SLOT)
    nn,r1,act,gp,w=feed_in(scalars,x,o,nm,(jnp.stack([wo]+[wi[:,c:c+D] for c in range(0,FF,D)],0),),FF)
    out,gfs,gmt=feed_out(scalars,nn,r1,act,gp,go,w,nm,(wt[None],))
    return qkv,low,wqkv,e,ot,rt,out,gfs,gmt,upq,upv,dnt

def shards(x,lengths,wq,wk,wv,wo,wi,wt,ag,ash,fg,fsh,qd,qu,vd,vu,go):
    n=device_count()
    valid=lengths[:,0]+lengths[:,1]+4
    me=(lax.axis_index("dp")*lax.axis_size("fsdp")+lax.axis_index("fsdp")).reshape(1)
    scalars=jnp.concatenate([me,valid]).astype(jnp.int32)
    forward=by_hops if n==32 and wq.shape[0]%8==0 else by_all_gather
    qkv,low,wqkv,e,ot,rt,out,gfs,gmt,upq,upv,dnt=forward(scalars,x,wq,wk,wv,wo,wi,wt,ag,ash,fg,fsh,qd,qu,vd,vu,go)
    d,gl,mine,other=attend_back(scalars,qkv,e,ot,rt,gmt,x,low,upq,upv)
    mine,other,gx=total_over_devices(mine,other,lambda: inputs_grad(gfs,d,gl,wqkv,dnt))
    qd,vd,qu,vu=finish(scalars,mine,other,1.0/(lengths.shape[0]*n))
    return out,gx,qd.T,qu,vd.T,vu

def solution(mesh):
    sp=P(AXES,None)
    return jax.shard_map(shards,mesh=mesh,in_specs=(sp,)*8+(P(),)*8+(sp,),
        out_specs=(sp,sp,P(),P(),P(),P()),check_vma=False)
```

profile of v0, /device:TPU:0, one launch (start us, length us, event | category | flops | bytes accessed | tf_op | source)
XLA Modules:
  0.0 150.3 jit_solution(15463243746088378479)
XLA Ops:
  1.7 2.1 %all-gather = bf16[144,768]{1,0:T(8,128)(2,1)S(1)} all-gather(bf16[72,768]{1,0:T(8,128)(2,1)S(1)} %pad_maximum_fusion.5), channel_id=2, replica_groups={{0,1},{2,3},{4,5},{6,7},{8,9},{10,11},{12,13},{14,15},{16,17},{18,19},{..., dimensions={0}, use_global_device_ids=true | all-gather | bytes 331776 | tf_op jit(solution)/shard_map/all_gather | solution.py:381
  3.9 5.0 %collective-permute-start.2 = (bf16[144,384]{1,0:T(8,128)(2,1)S(1)}, bf16[144,384]{1,0:T(8,128)(2,1)S(1)}, u32[]{:S(2)}, u32[]{:S(2)}) collective-permute-start(bf16[144,384]{1,0:T(8,128)(2,1)S(1)} %pad_maximum_fusion.6), channel_id=1, source_target_pairs={{0,24},{1,25},{2,26},{3,27},{4,28},{5,29},{6,30},{7,31},{8,16},{9,... | collective-permute-start | bytes 331784 | tf_op jit(solution)/shard_map/ppermute | solution.py:361
  9.5 2.0 %all-gather.3 = bf16[192,768]{1,0:T(8,128)(2,1)S(1)} all-gather(bf16[96,768]{1,0:T(8,128)(2,1)S(1)} %copy-done.9), channel_id=5, replica_groups={{0,1},{2,3},{4,5},{6,7},{8,9},{10,11},{12,13},{14,15},{16,17},{18,19},{..., dimensions={0}, use_global_device_ids=true | all-gather | bytes 442368 | tf_op jit(solution)/shard_map/all_gather | solution.py:381
  11.6 1.7 %collective-permute-start.3 = (bf16[192,384]{1,0:T(8,128)(2,1)S(1)}, bf16[192,384]{1,0:T(8,128)(2,1)S(1)}, u32[]{:S(2)}, u32[]{:S(2)}) collective-permute-start(bf16[192,384]{1,0:T(8,128)(2,1)S(1)} %bitcast.106), channel_id=1, source_target_pairs={{0,2},{1,5},{2,0},{3,7},{4,6},{5,1},{6,4},{7,3},{8,10},{9,13},{10,... | collective-permute-start | bytes 442376 | tf_op jit(solution)/shard_map/ppermute | solution.py:361
  13.6 1.9 %all-gather.1 = bf16[48,768]{1,0:T(8,128)(2,1)S(1)} all-gather(bf16[24,768]{1,0:T(8,128)(2,1)S(1)} %copy-done.11), channel_id=3, replica_groups={{0,1},{2,3},{4,5},{6,7},{8,9},{10,11},{12,13},{14,15},{16,17},{18,19},{..., dimensions={0}, use_global_device_ids=true | all-gather | bytes 110592 | tf_op jit(solution)/shard_map/all_gather | solution.py:381
  15.4 2.0 %all-gather.2 = bf16[48,3072]{1,0:T(8,128)(2,1)S(1)} all-gather(bf16[24,3072]{1,0:T(8,128)(2,1)S(1)} %copy-done.10), channel_id=4, replica_groups={{0,1},{2,3},{4,5},{6,7},{8,9},{10,11},{12,13},{14,15},{16,17},{18,19},{..., dimensions={0}, use_global_device_ids=true | all-gather | bytes 442368 | tf_op jit(solution)/shard_map/all_gather | solution.py:381
  18.5 1.6 %collective-permute-start.5 = (bf16[240,384]{1,0:T(8,128)(2,1)S(1)}, bf16[240,384]{1,0:T(8,128)(2,1)S(1)}, u32[]{:S(2)}, u32[]{:S(2)}) collective-permute-start(bf16[240,384]{1,0:T(8,128)(2,1)S(1)} %constant_dynamic-update-slice_fusion), channel_id=1, source_target_pairs={{0,16},{1,17},{2,18},{3,19},{4,20},{5,21},{6,22},{7,23},{8,24},{9,... | collective-permute-start | bytes 552968 | tf_op jit(solution)/shard_map/ppermute | solution.py:361
  21.6 2.1 %collective-permute-start.7 = (bf16[2,192,384]{2,1,0:T(8,128)(2,1)S(1)}, bf16[2,192,384]{2,1,0:T(8,128)(2,1)S(1)}, u32[]{:S(2)}, u32[]{:S(2)}) collective-permute-start(bf16[2,192,384]{2,1,0:T(8,128)(2,1)S(1)} %get-tuple-element.138), channel_id=1, source_target_pairs={{0,8},{1,9},{2,10},{3,11},{4,12},{5,13},{6,14},{7,15},{8,0},{9,1},... | collective-permute-start | bytes 884744 | tf_op jit(solution)/shard_map/ppermute | solution.py:361
  23.7 6.0 %collective-permute-done.5 = bf16[240,384]{1,0:T(8,128)(2,1)S(1)} collective-permute-done((bf16[240,384]{1,0:T(8,128)(2,1)S(1)}, bf16[240,384]{1,0:T(8,128)(2,1)S(1)}, u32[]{:S(2)}, u32[]{:S(2)}) %collective-permute-start.5) | collective-permute-done | bytes 184352 | tf_op jit(solution)/shard_map/ppermute | solution.py:361
  29.7 1.3 collective-permute-start.8
  31.9 1.5 collective-permute-start.11
  33.4 1.8 %low_rank.1 = (bf16[32,1024]{1,0:T(8,128)(2,1)S(1)}, f32[1024,768]{1,0:T(8,128)S(1)}, f32[1024,768]{1,0:T(8,128)S(1)}) custom-call(bf16[1024,768]{1,0:T(8,128)(2,1)S(1)} %copy-done.1, bf16[768,128]{1,0:T(8,128)(2,1)S(1)} %get-tuple-element.81.dn_ref, bf16[128,768]{1,0:T(8,128)(2,1)S(1)} %get-tuple-element.82.upq_ref, ...), custom_call_target="tpu_custom_call" | custom-call | flops 3300000000 | tf_op jit(solution)/shard_map/low_rank/pallas_call | solution.py:83
  35.3 6.4 %collective-permute-done.6 = bf16[2,240,384]{2,1,0:T(8,128)(2,1)S(1)} collective-permute-done((bf16[2,240,384]{2,1,0:T(8,128)(2,1)S(1)}, bf16[2,240,384]{2,1,0:T(8,128)(2,1)S(1)}, u32[]{:S(2)}, u32[]{:S(2)}) %collective-permute-start.6) | collective-permute-done | bytes 368672 | tf_op jit(solution)/shard_map/ppermute | solution.py:361
  42.4 1.6 %collective-permute-start.15 = (bf16[2,2,192,384]{3,2,0,1:T(8,128)(2,1)S(1)}, bf16[2,2,192,384]{3,2,0,1:T(8,128)(2,1)S(1)}, u32[]{:S(2)}, u32[]{:S(2)}) collective-permute-start(bf16[2,2,192,384]{3,2,0,1:T(8,128)(2,1)S(1)} %pad_maximum_fusion.1), channel_id=1, source_target_pairs={{0,16},{1,17},{2,18},{3,19},{4,20},{5,21},{6,22},{7,23},{8,24},{9,... | collective-permute-start | bytes 1769480 | tf_op jit(solution)/shard_map/ppermute | solution.py:361
  44.1 2.3 %collective-permute-done.11 = bf16[8,144,384]{2,1,0:T(8,128)(2,1)S(1)} collective-permute-done((bf16[8,144,384]{2,1,0:T(8,128)(2,1)S(1)}, bf16[8,144,384]{2,1,0:T(8,128)(2,1)S(1)}, u32[]{:S(2)}, u32[]{:S(2)}) %collective-permute-start.11) | collective-permute-done | bytes 884768 | tf_op jit(solution)/shard_map/ppermute | solution.py:361
  46.4 1.9 %collective-permute-start.13 = (bf16[8,144,384]{2,1,0:T(8,128)(2,1)S(1)}, bf16[8,144,384]{2,1,0:T(8,128)(2,1)S(1)}, u32[]{:S(2)}, u32[]{:S(2)}) collective-permute-start(bf16[8,144,384]{2,1,0:T(8,128)(2,1)S(1)} %collective-permute-done.11), channel_id=1, source_target_pairs={{0,1},{1,0},{2,3},{3,2},{4,5},{5,4},{6,7},{7,6},{8,9},{9,8},{10,11... | collective-permute-start | bytes 2654216 | tf_op jit(solution)/shard_map/ppermute | solution.py:361
  48.3 2.4 %collective-permute-done.9 = bf16[2,240,384]{2,1,0:T(8,128)(2,1)S(1)} collective-permute-done((bf16[2,240,384]{2,1,0:T(8,128)(2,1)S(1)}, bf16[2,240,384]{2,1,0:T(8,128)(2,1)S(1)}, u32[]{:S(2)}, u32[]{:S(2)}) %collective-permute-start.9) | collective-permute-done | bytes 368672 | tf_op jit(solution)/shard_map/ppermute | solution.py:361
  50.9 1.6 %collective-permute-start.10 = (bf16[8,240,384]{2,1,0:T(8,128)(2,1)S(1)}, bf16[8,240,384]{2,1,0:T(8,128)(2,1)S(1)}, u32[]{:S(2)}, u32[]{:S(2)}) collective-permute-start(bf16[8,240,384]{2,1,0:T(8,128)(2,1)S(1)} %constant_dynamic-update-slice_fusion.5), channel_id=1, source_target_pairs={{0,4},{1,3},{2,6},{3,1},{4,0},{5,7},{6,2},{7,5},{8,12},{9,11},{10,... | collective-permute-start | bytes 4423688 | tf_op jit(solution)/shard_map/ppermute | solution.py:361
  52.5 5.5 %project.1 = (bf16[1024,2304]{1,0:T(8,128)(2,1)S(1)}, bf16[3,768,768]{2,1,0:T(8,128)(2,1)}) custom-call(s32[3]{0:T(128)S(1)} %pad_add_fusion.sc_ref, bf16[1024,768]{1,0:T(8,128)(2,1)S(1)} %copy-done.1, f32[1024,768]{1,0:T(8,128)S(1)} %get-tuple-element.87.lq_ref, f32[1024,768]{1,0:T(8,128)S(1)} %get-tuple-element.88.lv_ref, ...), custom_call_target="tpu_custom_call" | custom-call | flops 8800000000 | tf_op jit(solution)/shard_map/project/pallas_call | solution.py:105
  58.0 13.0 %attend.1 = (bf16[24,512,512]{2,1,0:T(8,128)(2,1)}, bf16[1536,512]{1,0:T(8,128)(2,1)}, bf16[1024,768]{1,0:T(8,128)(2,1)S(1)}, f32[6,8,512]{2,1,0:T(8,128)}) custom-call(s32[3]{0:T(128)S(1)} %pad_add_fusion.sc_ref, bf16[1024,2304]{1,0:T(8,128)(2,1)S(1)} %get-tuple-element.92.qkv_ref.q_ref.k_ref.v_ref), custom_call_target="tpu_custom_call" | custom-call | flops 17600000000 | tf_op jit(solution)/shard_map/attend/pallas_call | solution.py:154
  73.1 1.3 collective-permute-done.17
  74.4 12.2 %feed_in.1 = (f32[1024,768]{1,0:T(8,128)S(1)}, f32[1024,128]{1,0:T(8,128)S(1)}, bf16[1024,3072]{1,0:T(8,128)(2,1)S(1)}, bf16[1024,3072]{1,0:T(8,128)(2,1)S(1)}, bf16[5,768,768]{2,1,0:T(8,128)(2,1)S(1)}) custom-call(s32[3]{0:T(128)S(1)} %pad_add_fusion.sc_ref, bf16[1024,768]{1,0:T(8,128)(2,1)S(1)} %copy-done.1, ...), custom_call_target="tpu_custom_call" | custom-call | flops 15399999488 | tf_op jit(solution)/shard_map/feed_in/pallas_call | solution.py:196
  86.6 1.7 %collective-permute-done.16 = bf16[8,192,384]{2,1,0:T(8,128)(2,1)S(1)} collective-permute-done((bf16[8,192,384]{2,1,0:T(8,128)(2,1)S(1)}, bf16[8,192,384]{2,1,0:T(8,128)(2,1)S(1)}, u32[]{:S(2)}, u32[]{:S(2)}) %collective-permute-start.16) | collective-permute-done | bytes 1179680 | tf_op jit(solution)/shard_map/ppermute | solution.py:361
  88.4 2.8 %collective-permute-done.19 = bf16[8,192,384]{2,1,0:T(8,128)(2,1)S(1)} collective-permute-done((bf16[8,192,384]{2,1,0:T(8,128)(2,1)S(1)}, bf16[8,192,384]{2,1,0:T(8,128)(2,1)S(1)}, u32[]{:S(2)}, u32[]{:S(2)}) %collective-permute-start.19) | collective-permute-done | bytes 1179680 | tf_op jit(solution)/shard_map/ppermute | solution.py:361
  91.2 20.9 %feed_out.1 = (bf16[1024,768]{1,0:T(8,128)(2,1)}, f32[1024,768]{1,0:T(8,128)S(1)}, bf16[768,1024]{1,0:T(8,128)(2,1)S(1)}, bf16[1024,3072]{1,0:T(8,128)(2,1)S(1)}) custom-call(s32[3]{0:T(128)S(1)} %pad_add_fusion.sc_ref, f32[1024,768]{1,0:T(8,128)S(1)} %get-tuple-element.100.n1_ref, ...), custom_call_target="tpu_custom_call", output_to_operand_aliasing={{3}: (3, {})} | custom-call | flops 26400000000 | tf_op jit(solution)/shard_map/feed_out/pallas_call | solution.py:239
  112.1 17.3 %attend_back.1 = (bf16[1024,2304]{1,0:T(8,128)(2,1)S(1)}, bf16[16,1024]{1,0:T(8,128)(2,1)S(1)}, f32[16,768]{1,0:T(8,128)S(1)}, f32[16,768]{1,0:T(8,128)S(1)}) custom-call(s32[3]{0:T(128)S(1)} %pad_add_fusion.sc_ref, bf16[1024,2304]{1,0:T(8,128)(2,1)} %copy-done.7, bf16[1024,2304]{1,0:T(8,128)(2,1)} %copy-done.7, bf16[1024,2304]{1,0:T(8,128)(2,1)} %copy-done.7, ...), custom_call_target="tpu_custom_call" | custom-call | flops 19800000512 | tf_op jit(solution)/shard_map/attend_back/pallas_call | solution.py:330
  130.8 1.4 collective-permute-start.23
  132.2 1.3 collective-permute-start.22
  134.3 1.6 %collective-permute-done.23 = f32[16,768]{1,0:T(8,128)S(1)} collective-permute-done((f32[16,768]{1,0:T(8,128)S(1)}, f32[16,768]{1,0:T(8,128)S(1)}, u32[]{:S(2)}, u32[]{:S(2)}) %collective-permute-start.23) | collective-permute-done | bytes 49184 | tf_op jit(solution)/shard_map/ppermute | solution.py:361
  137.6 2.4 %collective-permute-start.26 = (f32[16,768]{1,0:T(8,128)S(1)}, f32[16,768]{1,0:T(8,128)S(1)}, u32[]{:S(2)}, u32[]{:S(2)}) collective-permute-start(f32[16,768]{1,0:T(8,128)S(1)} %add_add_fusion.1), channel_id=1, source_target_pairs={{0,24},{1,25},{2,26},{3,27},{4,28},{5,29},{6,30},{7,31},{8,16},{9,... | collective-permute-start | bytes 147464 | tf_op jit(solution)/shard_map/ppermute | solution.py:361
  140.0 2.0 %collective-permute-start.24 = (f32[16,768]{1,0:T(8,128)S(1)}, f32[16,768]{1,0:T(8,128)S(1)}, u32[]{:S(2)}, u32[]{:S(2)}) collective-permute-start(f32[16,768]{1,0:T(8,128)S(1)} %add_add_fusion.1), channel_id=1, source_target_pairs={{0,8},{1,9},{2,10},{3,11},{4,12},{5,13},{6,14},{7,15},{8,0},{9,1},... | collective-permute-start | bytes 147464 | tf_op jit(solution)/shard_map/ppermute | solution.py:361
  142.1 5.7 %inputs_grad.1 = f32[1024,768]{1,0:T(8,128)} custom-call(f32[1024,768]{1,0:T(8,128)S(1)} %get-tuple-element.115.gfs_ref, bf16[1024,2304]{1,0:T(8,128)(2,1)S(1)} %get-tuple-element.116.d_ref, bf16[16,1024]{1,0:T(8,128)(2,1)S(1)} %get-tuple-element.117.gl, bf16[3,768,768]{2,1,0:T(8,128)(2,1)S(1)} %copy-done.6, bf16[16,768]{1,0:T(8,128)(2,1)S(1)} %get-tuple-element.119.dnt_ref), custom_call_target="tpu_custom_call" | custom-call | flops 7699999744 | tf_op jit(solution)/shard_map/inputs_grad/pallas_call | solution.py:351
  (128 shorter events, 14.8 us)
Async XLA Ops:
  0.6 14.8 %copy-start.10 = (bf16[24,3072]{1,0:T(8,128)(2,1)S(1)}, bf16[24,3072]{1,0:T(8,128)(2,1)}, u32[]{:S(2)}) copy-start(bf16[24,3072]{1,0:T(8,128)(2,1)} %param.23) | copy-start | bytes 442372
  3.9 14.0 %collective-permute-start.2 = (bf16[144,384]{1,0:T(8,128)(2,1)S(1)}, bf16[144,384]{1,0:T(8,128)(2,1)S(1)}, u32[]{:S(2)}, u32[]{:S(2)}) collective-permute-start(bf16[144,384]{1,0:T(8,128)(2,1)S(1)} %pad_maximum_fusion.6), channel_id=1, source_target_pairs={{0,24},{1,25},{2,26},{3,27},{4,28},{5,29},{6,30},{7,31},{8,16},{9,... | collective-permute-start | bytes 331784 | tf_op jit(solution)/shard_map/ppermute | solution.py:361
  8.9 9.6 %collective-permute-start.1 = (bf16[144,384]{1,0:T(8,128)(2,1)S(1)}, bf16[144,384]{1,0:T(8,128)(2,1)S(1)}, u32[]{:S(2)}, u32[]{:S(2)}) collective-permute-start(bf16[144,384]{1,0:T(8,128)(2,1)S(1)} %pad_maximum_fusion.6), channel_id=1, source_target_pairs={{0,16},{1,17},{2,18},{3,19},{4,20},{5,21},{6,22},{7,23},{8,24},{9,... | collective-permute-start | bytes 331784 | tf_op jit(solution)/shard_map/ppermute | solution.py:361
  8.9 9.6 %collective-permute-start = (bf16[144,384]{1,0:T(8,128)(2,1)S(1)}, bf16[144,384]{1,0:T(8,128)(2,1)S(1)}, u32[]{:S(2)}, u32[]{:S(2)}) collective-permute-start(bf16[144,384]{1,0:T(8,128)(2,1)S(1)} %pad_maximum_fusion.6), channel_id=1, source_target_pairs={{0,8},{1,9},{2,10},{3,11},{4,12},{5,13},{6,14},{7,15},{8,0},{9,1},... | collective-permute-start | bytes 331784 | tf_op jit(solution)/shard_map/ppermute | solution.py:361
  11.6 9.9 %collective-permute-start.3 = (bf16[192,384]{1,0:T(8,128)(2,1)S(1)}, bf16[192,384]{1,0:T(8,128)(2,1)S(1)}, u32[]{:S(2)}, u32[]{:S(2)}) collective-permute-start(bf16[192,384]{1,0:T(8,128)(2,1)S(1)} %bitcast.106), channel_id=1, source_target_pairs={{0,2},{1,5},{2,0},{3,7},{4,6},{5,1},{6,4},{7,3},{8,10},{9,13},{10,... | collective-permute-start | bytes 442376 | tf_op jit(solution)/shard_map/ppermute | solution.py:361
  18.5 11.1 %collective-permute-start.5 = (bf16[240,384]{1,0:T(8,128)(2,1)S(1)}, bf16[240,384]{1,0:T(8,128)(2,1)S(1)}, u32[]{:S(2)}, u32[]{:S(2)}) collective-permute-start(bf16[240,384]{1,0:T(8,128)(2,1)S(1)} %constant_dynamic-update-slice_fusion), channel_id=1, source_target_pairs={{0,16},{1,17},{2,18},{3,19},{4,20},{5,21},{6,22},{7,23},{8,24},{9,... | collective-permute-start | bytes 552968 | tf_op jit(solution)/shard_map/ppermute | solution.py:361
  20.2 9.4 %collective-permute-start.4 = (bf16[4,144,384]{2,1,0:T(8,128)(2,1)S(1)}, bf16[4,144,384]{2,1,0:T(8,128)(2,1)S(1)}, u32[]{:S(2)}, u32[]{:S(2)}) collective-permute-start(bf16[4,144,384]{2,1,0:T(8,128)(2,1)S(1)} %pad_maximum_fusion.2), channel_id=1, source_target_pairs={{0,2},{1,5},{2,0},{3,7},{4,6},{5,1},{6,4},{7,3},{8,10},{9,13},{10,... | collective-permute-start | bytes 1327112 | tf_op jit(solution)/shard_map/ppermute | solution.py:361
  21.6 13.7 %collective-permute-start.7 = (bf16[2,192,384]{2,1,0:T(8,128)(2,1)S(1)}, bf16[2,192,384]{2,1,0:T(8,128)(2,1)S(1)}, u32[]{:S(2)}, u32[]{:S(2)}) collective-permute-start(bf16[2,192,384]{2,1,0:T(8,128)(2,1)S(1)} %get-tuple-element.138), channel_id=1, source_target_pairs={{0,8},{1,9},{2,10},{3,11},{4,12},{5,13},{6,14},{7,15},{8,0},{9,1},... | collective-permute-start | bytes 884744 | tf_op jit(solution)/shard_map/ppermute | solution.py:361
  29.7 18.6 %collective-permute-start.8 = (bf16[2,240,384]{2,1,0:T(8,128)(2,1)S(1)}, bf16[2,240,384]{2,1,0:T(8,128)(2,1)S(1)}, u32[]{:S(2)}, u32[]{:S(2)}) collective-permute-start(bf16[2,240,384]{2,1,0:T(8,128)(2,1)S(1)} %pad_maximum_fusion.3), channel_id=1, source_target_pairs={{0,2},{1,5},{2,0},{3,7},{4,6},{5,1},{6,4},{7,3},{8,10},{9,13},{10,... | collective-permute-start | bytes 1105928 | tf_op jit(solution)/shard_map/ppermute | solution.py:361
  31.0 10.7 %collective-permute-start.6 = (bf16[2,240,384]{2,1,0:T(8,128)(2,1)S(1)}, bf16[2,240,384]{2,1,0:T(8,128)(2,1)S(1)}, u32[]{:S(2)}, u32[]{:S(2)}) collective-permute-start(bf16[2,240,384]{2,1,0:T(8,128)(2,1)S(1)} %pad_maximum_fusion.3), channel_id=1, source_target_pairs={{0,8},{1,9},{2,10},{3,11},{4,12},{5,13},{6,14},{7,15},{8,0},{9,1},... | collective-permute-start | bytes 1105928 | tf_op jit(solution)/shard_map/ppermute | solution.py:361
  31.8 12.3 %collective-permute-start.12 = (bf16[8,144,384]{2,1,0:T(8,128)(2,1)S(1)}, bf16[8,144,384]{2,1,0:T(8,128)(2,1)S(1)}, u32[]{:S(2)}, u32[]{:S(2)}) collective-permute-start(bf16[8,144,384]{2,1,0:T(8,128)(2,1)S(1)} %constant_dynamic-update-slice_fusion.18), channel_id=1, source_target_pairs={{0,1},{1,0},{2,3},{3,2},{4,5},{5,4},{6,7},{7,6},{8,9},{9,8},{10,11... | collective-permute-start | bytes 2654216 | tf_op jit(solution)/shard_map/ppermute | solution.py:361
  31.9 14.5 %collective-permute-start.11 = (bf16[8,144,384]{2,1,0:T(8,128)(2,1)S(1)}, bf16[8,144,384]{2,1,0:T(8,128)(2,1)S(1)}, u32[]{:S(2)}, u32[]{:S(2)}) collective-permute-start(bf16[8,144,384]{2,1,0:T(8,128)(2,1)S(1)} %constant_dynamic-update-slice_fusion.18), channel_id=1, source_target_pairs={{0,4},{1,3},{2,6},{3,1},{4,0},{5,7},{6,2},{7,5},{8,12},{9,11},{10,... | collective-permute-start | bytes 2654216 | tf_op jit(solution)/shard_map/ppermute | solution.py:361
  41.7 9.0 %collective-permute-start.9 = (bf16[2,240,384]{2,1,0:T(8,128)(2,1)S(1)}, bf16[2,240,384]{2,1,0:T(8,128)(2,1)S(1)}, u32[]{:S(2)}, u32[]{:S(2)}) collective-permute-start(bf16[2,240,384]{2,1,0:T(8,128)(2,1)S(1)} %collective-permute-done.6), channel_id=1, source_target_pairs={{0,2},{1,5},{2,0},{3,7},{4,6},{5,1},{6,4},{7,3},{8,10},{9,13},{10,... | collective-permute-start | bytes 1105928 | tf_op jit(solution)/shard_map/ppermute | solution.py:361
  42.4 28.7 %collective-permute-start.15 = (bf16[2,2,192,384]{3,2,0,1:T(8,128)(2,1)S(1)}, bf16[2,2,192,384]{3,2,0,1:T(8,128)(2,1)S(1)}, u32[]{:S(2)}, u32[]{:S(2)}) collective-permute-start(bf16[2,2,192,384]{3,2,0,1:T(8,128)(2,1)S(1)} %pad_maximum_fusion.1), channel_id=1, source_target_pairs={{0,16},{1,17},{2,18},{3,19},{4,20},{5,21},{6,22},{7,23},{8,24},{9,... | collective-permute-start | bytes 1769480 | tf_op jit(solution)/shard_map/ppermute | solution.py:361
  46.4 6.1 %collective-permute-start.13 = (bf16[8,144,384]{2,1,0:T(8,128)(2,1)S(1)}, bf16[8,144,384]{2,1,0:T(8,128)(2,1)S(1)}, u32[]{:S(2)}, u32[]{:S(2)}) collective-permute-start(bf16[8,144,384]{2,1,0:T(8,128)(2,1)S(1)} %collective-permute-done.11), channel_id=1, source_target_pairs={{0,1},{1,0},{2,3},{3,2},{4,5},{5,4},{6,7},{7,6},{8,9},{9,8},{10,11... | collective-permute-start | bytes 2654216 | tf_op jit(solution)/shard_map/ppermute | solution.py:361
  50.8 20.2 %collective-permute-start.14 = (bf16[8,240,384]{2,1,0:T(8,128)(2,1)S(1)}, bf16[8,240,384]{2,1,0:T(8,128)(2,1)S(1)}, u32[]{:S(2)}, u32[]{:S(2)}) collective-permute-start(bf16[8,240,384]{2,1,0:T(8,128)(2,1)S(1)} %constant_dynamic-update-slice_fusion.5), channel_id=1, source_target_pairs={{0,1},{1,0},{2,3},{3,2},{4,5},{5,4},{6,7},{7,6},{8,9},{9,8},{10,11... | collective-permute-start | bytes 4423688 | tf_op jit(solution)/shard_map/ppermute | solution.py:361
  50.9 20.1 %collective-permute-start.10 = (bf16[8,240,384]{2,1,0:T(8,128)(2,1)S(1)}, bf16[8,240,384]{2,1,0:T(8,128)(2,1)S(1)}, u32[]{:S(2)}, u32[]{:S(2)}) collective-permute-start(bf16[8,240,384]{2,1,0:T(8,128)(2,1)S(1)} %constant_dynamic-update-slice_fusion.5), channel_id=1, source_target_pairs={{0,4},{1,3},{2,6},{3,1},{4,0},{5,7},{6,2},{7,5},{8,12},{9,11},{10,... | collective-permute-start | bytes 4423688 | tf_op jit(solution)/shard_map/ppermute | solution.py:361
  71.1 3.3 %collective-permute-start.17 = (bf16[8,240,384]{2,1,0:T(8,128)(2,1)S(1)}, bf16[8,240,384]{2,1,0:T(8,128)(2,1)S(1)}, u32[]{:S(2)}, u32[]{:S(2)}) collective-permute-start(bf16[8,240,384]{2,1,0:T(8,128)(2,1)S(1)} %collective-permute-done.10), channel_id=1, source_target_pairs={{0,1},{1,0},{2,3},{3,2},{4,5},{5,4},{6,7},{7,6},{8,9},{9,8},{10,11... | collective-permute-start | bytes 4423688 | tf_op jit(solution)/shard_map/ppermute | solution.py:361
  71.6 15.0 %collective-permute-start.18 = (bf16[8,192,384]{2,1,0:T(8,128)(2,1)S(1)}, bf16[8,192,384]{2,1,0:T(8,128)(2,1)S(1)}, u32[]{:S(2)}, u32[]{:S(2)}) collective-permute-start(bf16[8,192,384]{2,1,0:T(8,128)(2,1)S(1)} %bitcast.68), channel_id=1, source_target_pairs={{0,1},{1,0},{2,3},{3,2},{4,5},{5,4},{6,7},{7,6},{8,9},{9,8},{10,11... | collective-permute-start | bytes 3538952 | tf_op jit(solution)/shard_map/ppermute | solution.py:361
  72.2 16.2 %collective-permute-start.16 = (bf16[8,192,384]{2,1,0:T(8,128)(2,1)S(1)}, bf16[8,192,384]{2,1,0:T(8,128)(2,1)S(1)}, u32[]{:S(2)}, u32[]{:S(2)}) collective-permute-start(bf16[8,192,384]{2,1,0:T(8,128)(2,1)S(1)} %bitcast.69), channel_id=1, source_target_pairs={{0,4},{1,3},{2,6},{3,1},{4,0},{5,7},{6,2},{7,5},{8,12},{9,11},{10,... | collective-permute-start | bytes 3538952 | tf_op jit(solution)/shard_map/ppermute | solution.py:361
  74.4 16.8 %copy-start = (bf16[1024,768]{1,0:T(8,128)(2,1)S(1)}, bf16[1024,768]{1,0:T(8,128)(2,1)}, u32[]{:S(2)}) copy-start(bf16[1024,768]{1,0:T(8,128)(2,1)} %go_ref.1) | copy-start | bytes 4718596
  88.4 2.8 %collective-permute-start.19 = (bf16[8,192,384]{2,1,0:T(8,128)(2,1)S(1)}, bf16[8,192,384]{2,1,0:T(8,128)(2,1)S(1)}, u32[]{:S(2)}, u32[]{:S(2)}) collective-permute-start(bf16[8,192,384]{2,1,0:T(8,128)(2,1)S(1)} %collective-permute-done.16), channel_id=1, source_target_pairs={{0,1},{1,0},{2,3},{3,2},{4,5},{5,4},{6,7},{7,6},{8,9},{9,8},{10,11... | collective-permute-start | bytes 3538952 | tf_op jit(solution)/shard_map/ppermute | solution.py:361
  91.2 20.9 %copy-start.8 = (f32[6,8,512]{2,1,0:T(8,128)S(1)}, f32[6,8,512]{2,1,0:T(8,128)}, u32[]{:S(2)}) copy-start(f32[6,8,512]{2,1,0:T(8,128)} %get-tuple-element.110.rt_ref) | copy-start | bytes 294916
  112.1 29.9 %copy-start.6 = (bf16[3,768,768]{2,1,0:T(8,128)(2,1)S(1)}, bf16[3,768,768]{2,1,0:T(8,128)(2,1)}, u32[]{:S(2)}) copy-start(bf16[3,768,768]{2,1,0:T(8,128)(2,1)} %get-tuple-element.118.w_ref) | copy-start | bytes 10616836
  129.4 1.3 collective-permute-start.20
  130.8 5.1 %collective-permute-start.23 = (f32[16,768]{1,0:T(8,128)S(1)}, f32[16,768]{1,0:T(8,128)S(1)}, u32[]{:S(2)}, u32[]{:S(2)}) collective-permute-start(f32[16,768]{1,0:T(8,128)S(1)} %add.63), channel_id=1, source_target_pairs={{0,6},{1,7},{2,4},{3,5},{4,2},{5,3},{6,0},{7,1},{8,14},{9,15},{10,... | collective-permute-start | bytes 147464 | tf_op jit(solution)/shard_map/ppermute | solution.py:361
  132.2 4.4 %collective-permute-start.22 = (f32[16,768]{1,0:T(8,128)S(1)}, f32[16,768]{1,0:T(8,128)S(1)}, u32[]{:S(2)}, u32[]{:S(2)}) collective-permute-start(f32[16,768]{1,0:T(8,128)S(1)} %add.63), channel_id=1, source_target_pairs={{0,4},{1,5},{2,6},{3,7},{4,0},{5,1},{6,2},{7,3},{8,12},{9,13},{10,... | collective-permute-start | bytes 147464 | tf_op jit(solution)/shard_map/ppermute | solution.py:361
  133.5 4.1 %collective-permute-start.21 = (f32[16,768]{1,0:T(8,128)S(1)}, f32[16,768]{1,0:T(8,128)S(1)}, u32[]{:S(2)}, u32[]{:S(2)}) collective-permute-start(f32[16,768]{1,0:T(8,128)S(1)} %add.63), channel_id=1, source_target_pairs={{0,2},{1,3},{2,0},{3,1},{4,6},{5,7},{6,4},{7,5},{8,10},{9,11},{10,... | collective-permute-start | bytes 147464 | tf_op jit(solution)/shard_map/ppermute | solution.py:361
  137.6 10.2 %collective-permute-start.26 = (f32[16,768]{1,0:T(8,128)S(1)}, f32[16,768]{1,0:T(8,128)S(1)}, u32[]{:S(2)}, u32[]{:S(2)}) collective-permute-start(f32[16,768]{1,0:T(8,128)S(1)} %add_add_fusion.1), channel_id=1, source_target_pairs={{0,24},{1,25},{2,26},{3,27},{4,28},{5,29},{6,30},{7,31},{8,16},{9,... | collective-permute-start | bytes 147464 | tf_op jit(solution)/shard_map/ppermute | solution.py:361
  140.0 7.8 %collective-permute-start.25 = (f32[16,768]{1,0:T(8,128)S(1)}, f32[16,768]{1,0:T(8,128)S(1)}, u32[]{:S(2)}, u32[]{:S(2)}) collective-permute-start(f32[16,768]{1,0:T(8,128)S(1)} %add_add_fusion.1), channel_id=1, source_target_pairs={{0,16},{1,17},{2,18},{3,19},{4,20},{5,21},{6,22},{7,23},{8,24},{9,... | collective-permute-start | bytes 147464 | tf_op jit(solution)/shard_map/ppermute | solution.py:361
  140.0 7.8 %collective-permute-start.24 = (f32[16,768]{1,0:T(8,128)S(1)}, f32[16,768]{1,0:T(8,128)S(1)}, u32[]{:S(2)}, u32[]{:S(2)}) collective-permute-start(f32[16,768]{1,0:T(8,128)S(1)} %add_add_fusion.1), channel_id=1, source_target_pairs={{0,8},{1,9},{2,10},{3,11},{4,12},{5,13},{6,14},{7,15},{8,0},{9,1},... | collective-permute-start | bytes 147464 | tf_op jit(solution)/shard_map/ppermute | solution.py:361
  147.8 1.3 collective-permute-start.27
  (13 other events, 165.9 us)
where the time goes:
time: 150 us
  Pallas kernels  77.7 us (52%)
  starting transfers between devices  31.3 us (21%)
  waiting for transfers between devices  29.2 us (19%)
  blocking collectives  7.94 us (5%)
  other arithmetic  1.65 us (1%)
    ppermute x28, starting transfers between devices, permute(): lax.ppermute(v, AXES, [(i, target(i)) for i in range(device_count())])  31.3 us
    ppermute x28, waiting for transfers between devices, permute(): lax.ppermute(v, AXES, [(i, target(i)) for i in range(device_count())])  29.2 us
    pallas_call x1, Pallas kernels, feed_out(): pl.pallas_call(feed_out_kernel, in_specs=[SCALARS] + [HELD] * 7 + [ANY] *...  20.9 us
    pallas_call x1, Pallas kernels, attend_back(): pl.pallas_call(attend_back_kernel, grid=(S, J), in_specs=[SCALARS, *[pl.B...  17.3 us
    pallas_call x1, Pallas kernels, attend(): pl.pallas_call(attend_kernel, grid=(slots, J), in_specs=[SCALARS, HELD],...  13 us
    pallas_call x1, Pallas kernels, feed_in(): pl.pallas_call(feed_in_kernel, grid=(rows // SLOT,), in_specs=[SCALARS, H...  12.2 us
    all_gather x4, blocking collectives, core_pair(): lax.all_gather(v, 'fsdp', axis=0, tiled=False, axis_index_groups=groups)  7.94 us
    pallas_call x1, Pallas kernels, inputs_grad(): pl.pallas_call(inputs_kernel, grid=(rows // SLOT,), in_specs=[row, HELD,...  5.72 us
  transfers between devices with their start and end apart: 28, of which 13 were waited for; matrix products, arithmetic and copies ran while one was open for 1% of the time, Pallas kernels for 26%

commit v1 on v0

--- a/solution.py
+++ b/solution.py
@@ -337,21 +337,19 @@
         scratch_shapes=[pltpu.VMEM((16,SLOT),F32),pltpu.VMEM((32,D),F32)],
         compiler_params=params(LIM["attend_back"]),cost_estimate=takes(18),name="attend_back")(scalars,far(qkv),far(qkv),far(qkv),far(e),far(ot),rt,gmt,x,low,upq,upv)
 
-def inputs_kernel(gfs_ref,d_ref,gl,w_ref,dnt_ref,out_ref):
-    T=gfs_ref.shape[0]
-    rows=pl.ds(pl.multiple_of(pl.program_id(0)*T,T),T)
+def inputs_kernel(s,gfs_ref,d_ref,gl,w_ref,dnt_ref,*rest):
     D=gfs_ref.shape[1]
-    v=gfs_ref[...]+dg(gl[...],dnt_ref[...],0,0)
+    rows=slice(s*SLOT,(s+1)*SLOT)
+    v=gfs_ref[rows,:]+dg(gl[...],dnt_ref[...],0,0)
     for t in range(3): v=v+dg(d_ref[rows,t*D:(t+1)*D],w_ref[t],1,1)
-    out_ref[...]=v
-
-def inputs_grad(gfs,d,gl,w,dnt):
+    rest[-1][...]=v
+
+def inputs_grad(s,gfs,d,gl,w,dnt,into=()):
     rows,D=gfs.shape
-    row=pl.BlockSpec((SLOT,D),lambda i:(i,0))
-    return pl.pallas_call(inputs_kernel,grid=(rows//SLOT,),
-        in_specs=[row,HELD,pl.BlockSpec((16,SLOT),lambda i:(0,i)),HELD,HELD],
-        out_specs=row,out_shape=sd((rows,D),F32),
-        compiler_params=params(LIM["inputs_grad"]),cost_estimate=takes(7),name="inputs_grad")(gfs,d,gl,w,dnt)
+    return pl.pallas_call(functools.partial(inputs_kernel,s),grid=(1,),
+        in_specs=[HELD,HELD,pl.BlockSpec((16,SLOT),lambda i:(0,s)),HELD,HELD]+[ANY]*len(into),
+        out_specs=pl.BlockSpec((SLOT,D),lambda i:(s,0)),out_shape=sd((rows,D),F32),input_output_aliases={5:0} if into else {},
+        compiler_params=params(LIM["inputs_grad"]),cost_estimate=takes(3),name="inputs_grad")(gfs,d,gl,w,dnt,*into)
 
 
 def device_count():
@@ -385,13 +383,14 @@
     half=both.shape[2]//2
     return lax.dynamic_slice_in_dim(both,c*half,half,axis=2).reshape(-1,half)
 
-def total_over_devices(mine,other,meanwhile):
+def total_over_devices(mine,other,beside_near,beside_z):
     n=device_count()
     mine=mine+exchange(other,1)
     got=[exchange(mine,m) for m in range(2,n//4,2)]
+    got,done=tie(got,beside_near())
     for g in got: mine=mine+g
     got=[exchange(mine,m) for m in (n//4,n//2,3*n//4)]
-    got,done=tie(got,meanwhile())
+    got,done=tie(got,beside_z(done))
     for g in got: mine=mine+g
     return mine,exchange(mine,1),done
 
@@ -476,7 +475,10 @@
     forward=by_hops if n==32 and wq.shape[0]%8==0 else by_all_gather
     qkv,low,wqkv,e,ot,rt,out,gfs,gmt,upq,upv,dnt=forward(scalars,x,wq,wk,wv,wo,wi,wt,ag,ash,fg,fsh,qd,qu,vd,vu,go)
     d,gl,mine,other=attend_back(scalars,qkv,e,ot,rt,gmt,x,low,upq,upv)
-    mine,other,gx=total_over_devices(mine,other,lambda: inputs_grad(gfs,d,gl,wqkv,dnt))
+    def later_rows(gx):
+        for s in range(1,x.shape[0]//SLOT): gx=inputs_grad(s,gfs,d,gl,wqkv,dnt,(gx,))
+        return gx
+    mine,other,gx=total_over_devices(mine,other,lambda: inputs_grad(0,gfs,d,gl,wqkv,dnt),later_rows)
     qd,vd,qu,vu=finish(scalars,mine,other,1.0/(lengths.shape[0]*n))
     return out,gx,qd.T,qu,vd.T,vu
 

time: 150 us -> 149 us (level)
  waiting for transfers between devices: 29.2 us -> 26.1 us
  Pallas kernels: 77.7 us -> 79.2 us
    ppermute x28, waiting for transfers between devices: 29.2 us -> 26.1 us  [permute(): lax.ppermute(v, AXES, [(i, target(i)) for i in range(device_count())])]
    pallas_call x1 -> x2, Pallas kernels: 5.72 us -> 6.89 us  [inputs_grad(): pl.pallas_call(functools.partial(inputs_kernel, s), grid=(1,), in_specs=[...]
  transfers between devices with their start and end apart: 28 -> 28, of which waited for: 13 -> 11; matrix products, arithmetic and copies ran while one was open for 1% -> 1% of each run, Pallas kernels for 26% -> 27%
where the time goes in v1:
time: 149 us
  Pallas kernels  79.2 us (53%)
  starting transfers between devices  31.3 us (21%)
  waiting for transfers between devices  26.1 us (18%)
  blocking collectives  7.94 us (5%)
  other arithmetic  1.65 us (1%)
    ppermute x28, starting transfers between devices, permute(): lax.ppermute(v, AXES, [(i, target(i)) for i in range(device_count())])  31.3 us
    ppermute x28, waiting for transfers between devices, permute(): lax.ppermute(v, AXES, [(i, target(i)) for i in range(device_count())])  26.1 us
    pallas_call x1, Pallas kernels, feed_out(): pl.pallas_call(feed_out_kernel, in_specs=[SCALARS] + [HELD] * 7 + [ANY] *...  21.1 us
    pallas_call x1, Pallas kernels, attend_back(): pl.pallas_call(attend_back_kernel, grid=(S, J), in_specs=[SCALARS, *[pl.B...  17.3 us
    pallas_call x1, Pallas kernels, attend(): pl.pallas_call(attend_kernel, grid=(slots, J), in_specs=[SCALARS, HELD],...  13 us
    pallas_call x1, Pallas kernels, feed_in(): pl.pallas_call(feed_in_kernel, grid=(rows // SLOT,), in_specs=[SCALARS, H...  12.2 us
    all_gather x4, blocking collectives, core_pair(): lax.all_gather(v, 'fsdp', axis=0, tiled=False, axis_index_groups=groups)  7.94 us
    pallas_call x2, Pallas kernels, inputs_grad(): pl.pallas_call(functools.partial(inputs_kernel, s), grid=(1,), in_specs=[...  6.89 us
  transfers between devices with their start and end apart: 28, of which 11 were waited for; matrix products, arithmetic and copies ran while one was open for 1% of the time, Pallas kernels for 27%

profile of v1, /device:TPU:0, one launch (start us, length us, event | category | flops | bytes accessed | tf_op | source)
XLA Modules:
  0.0 148.7 jit_solution(13854272240177826558)
XLA Ops:
  1.7 2.1 %all-gather = bf16[144,768]{1,0:T(8,128)(2,1)S(1)} all-gather(bf16[72,768]{1,0:T(8,128)(2,1)S(1)} %pad_maximum_fusion.5), channel_id=2, replica_groups={{0,1},{2,3},{4,5},{6,7},{8,9},{10,11},{12,13},{14,15},{16,17},{18,19},{..., dimensions={0}, use_global_device_ids=true | all-gather | bytes 331776 | tf_op jit(solution)/shard_map/all_gather | solution.py:379
  3.9 5.0 %collective-permute-start.2 = (bf16[144,384]{1,0:T(8,128)(2,1)S(1)}, bf16[144,384]{1,0:T(8,128)(2,1)S(1)}, u32[]{:S(2)}, u32[]{:S(2)}) collective-permute-start(bf16[144,384]{1,0:T(8,128)(2,1)S(1)} %pad_maximum_fusion.6), channel_id=1, source_target_pairs={{0,24},{1,25},{2,26},{3,27},{4,28},{5,29},{6,30},{7,31},{8,16},{9,... | collective-permute-start | bytes 331784 | tf_op jit(solution)/shard_map/ppermute | solution.py:359
  9.5 2.0 %all-gather.3 = bf16[192,768]{1,0:T(8,128)(2,1)S(1)} all-gather(bf16[96,768]{1,0:T(8,128)(2,1)S(1)} %copy-done.9), channel_id=5, replica_groups={{0,1},{2,3},{4,5},{6,7},{8,9},{10,11},{12,13},{14,15},{16,17},{18,19},{..., dimensions={0}, use_global_device_ids=true | all-gather | bytes 442368 | tf_op jit(solution)/shard_map/all_gather | solution.py:379
  11.6 1.7 %collective-permute-start.3 = (bf16[192,384]{1,0:T(8,128)(2,1)S(1)}, bf16[192,384]{1,0:T(8,128)(2,1)S(1)}, u32[]{:S(2)}, u32[]{:S(2)}) collective-permute-start(bf16[192,384]{1,0:T(8,128)(2,1)S(1)} %bitcast.106), channel_id=1, source_target_pairs={{0,2},{1,5},{2,0},{3,7},{4,6},{5,1},{6,4},{7,3},{8,10},{9,13},{10,... | collective-permute-start | bytes 442376 | tf_op jit(solution)/shard_map/ppermute | solution.py:359
  13.6 1.9 %all-gather.1 = bf16[48,768]{1,0:T(8,128)(2,1)S(1)} all-gather(bf16[24,768]{1,0:T(8,128)(2,1)S(1)} %copy-done.11), channel_id=3, replica_groups={{0,1},{2,3},{4,5},{6,7},{8,9},{10,11},{12,13},{14,15},{16,17},{18,19},{..., dimensions={0}, use_global_device_ids=true | all-gather | bytes 110592 | tf_op jit(solution)/shard_map/all_gather | solution.py:379
  15.4 2.0 %all-gather.2 = bf16[48,3072]{1,0:T(8,128)(2,1)S(1)} all-gather(bf16[24,3072]{1,0:T(8,128)(2,1)S(1)} %copy-done.10), channel_id=4, replica_groups={{0,1},{2,3},{4,5},{6,7},{8,9},{10,11},{12,13},{14,15},{16,17},{18,19},{..., dimensions={0}, use_global_device_ids=true | all-gather | bytes 442368 | tf_op jit(solution)/shard_map/all_gather | solution.py:379
  18.5 1.6 %collective-permute-start.5 = (bf16[240,384]{1,0:T(8,128)(2,1)S(1)}, bf16[240,384]{1,0:T(8,128)(2,1)S(1)}, u32[]{:S(2)}, u32[]{:S(2)}) collective-permute-start(bf16[240,384]{1,0:T(8,128)(2,1)S(1)} %constant_dynamic-update-slice_fusion), channel_id=1, source_target_pairs={{0,16},{1,17},{2,18},{3,19},{4,20},{5,21},{6,22},{7,23},{8,24},{9,... | collective-permute-start | bytes 552968 | tf_op jit(solution)/shard_map/ppermute | solution.py:359
  21.6 2.1 %collective-permute-start.7 = (bf16[2,192,384]{2,1,0:T(8,128)(2,1)S(1)}, bf16[2,192,384]{2,1,0:T(8,128)(2,1)S(1)}, u32[]{:S(2)}, u32[]{:S(2)}) collective-permute-start(bf16[2,192,384]{2,1,0:T(8,128)(2,1)S(1)} %get-tuple-element.146), channel_id=1, source_target_pairs={{0,8},{1,9},{2,10},{3,11},{4,12},{5,13},{6,14},{7,15},{8,0},{9,1},... | collective-permute-start | bytes 884744 | tf_op jit(solution)/shard_map/ppermute | solution.py:359
  23.7 6.0 %collective-permute-done.5 = bf16[240,384]{1,0:T(8,128)(2,1)S(1)} collective-permute-done((bf16[240,384]{1,0:T(8,128)(2,1)S(1)}, bf16[240,384]{1,0:T(8,128)(2,1)S(1)}, u32[]{:S(2)}, u32[]{:S(2)}) %collective-permute-start.5) | collective-permute-done | bytes 184352 | tf_op jit(solution)/shard_map/ppermute | solution.py:359
  29.7 1.3 collective-permute-start.8
  31.9 1.5 collective-permute-start.11
  33.4 1.8 %low_rank.1 = (bf16[32,1024]{1,0:T(8,128)(2,1)S(1)}, f32[1024,768]{1,0:T(8,128)S(1)}, f32[1024,768]{1,0:T(8,128)S(1)}) custom-call(bf16[1024,768]{1,0:T(8,128)(2,1)S(1)} %copy-done.2, bf16[768,128]{1,0:T(8,128)(2,1)S(1)} %get-tuple-element.85.dn_ref, bf16[128,768]{1,0:T(8,128)(2,1)S(1)} %get-tuple-element.86.upq_ref, ...), custom_call_target="tpu_custom_call" | custom-call | flops 3300000000 | tf_op jit(solution)/shard_map/low_rank/pallas_call | solution.py:83
  35.3 6.4 %collective-permute-done.6 = bf16[2,240,384]{2,1,0:T(8,128)(2,1)S(1)} collective-permute-done((bf16[2,240,384]{2,1,0:T(8,128)(2,1)S(1)}, bf16[2,240,384]{2,1,0:T(8,128)(2,1)S(1)}, u32[]{:S(2)}, u32[]{:S(2)}) %collective-permute-start.6) | collective-permute-done | bytes 368672 | tf_op jit(solution)/shard_map/ppermute | solution.py:359
  42.4 1.6 %collective-permute-start.15 = (bf16[2,2,192,384]{3,2,0,1:T(8,128)(2,1)S(1)}, bf16[2,2,192,384]{3,2,0,1:T(8,128)(2,1)S(1)}, u32[]{:S(2)}, u32[]{:S(2)}) collective-permute-start(bf16[2,2,192,384]{3,2,0,1:T(8,128)(2,1)S(1)} %pad_maximum_fusion.1), channel_id=1, source_target_pairs={{0,16},{1,17},{2,18},{3,19},{4,20},{5,21},{6,22},{7,23},{8,24},{9,... | collective-permute-start | bytes 1769480 | tf_op jit(solution)/shard_map/ppermute | solution.py:359
  44.1 2.3 %collective-permute-done.11 = bf16[8,144,384]{2,1,0:T(8,128)(2,1)S(1)} collective-permute-done((bf16[8,144,384]{2,1,0:T(8,128)(2,1)S(1)}, bf16[8,144,384]{2,1,0:T(8,128)(2,1)S(1)}, u32[]{:S(2)}, u32[]{:S(2)}) %collective-permute-start.11) | collective-permute-done | bytes 884768 | tf_op jit(solution)/shard_map/ppermute | solution.py:359
  46.4 1.9 %collective-permute-start.13 = (bf16[8,144,384]{2,1,0:T(8,128)(2,1)S(1)}, bf16[8,144,384]{2,1,0:T(8,128)(2,1)S(1)}, u32[]{:S(2)}, u32[]{:S(2)}) collective-permute-start(bf16[8,144,384]{2,1,0:T(8,128)(2,1)S(1)} %collective-permute-done.11), channel_id=1, source_target_pairs={{0,1},{1,0},{2,3},{3,2},{4,5},{5,4},{6,7},{7,6},{8,9},{9,8},{10,11... | collective-permute-start | bytes 2654216 | tf_op jit(solution)/shard_map/ppermute | solution.py:359
  48.3 2.4 %collective-permute-done.9 = bf16[2,240,384]{2,1,0:T(8,128)(2,1)S(1)} collective-permute-done((bf16[2,240,384]{2,1,0:T(8,128)(2,1)S(1)}, bf16[2,240,384]{2,1,0:T(8,128)(2,1)S(1)}, u32[]{:S(2)}, u32[]{:S(2)}) %collective-permute-start.9) | collective-permute-done | bytes 368672 | tf_op jit(solution)/shard_map/ppermute | solution.py:359
  50.9 1.6 %collective-permute-start.10 = (bf16[8,240,384]{2,1,0:T(8,128)(2,1)S(1)}, bf16[8,240,384]{2,1,0:T(8,128)(2,1)S(1)}, u32[]{:S(2)}, u32[]{:S(2)}) collective-permute-start(bf16[8,240,384]{2,1,0:T(8,128)(2,1)S(1)} %constant_dynamic-update-slice_fusion.5), channel_id=1, source_target_pairs={{0,4},{1,3},{2,6},{3,1},{4,0},{5,7},{6,2},{7,5},{8,12},{9,11},{10,... | collective-permute-start | bytes 4423688 | tf_op jit(solution)/shard_map/ppermute | solution.py:359
  52.5 5.6 %project.1 = (bf16[1024,2304]{1,0:T(8,128)(2,1)S(1)}, bf16[3,768,768]{2,1,0:T(8,128)(2,1)}) custom-call(s32[3]{0:T(128)S(1)} %pad_add_fusion.sc_ref, bf16[1024,768]{1,0:T(8,128)(2,1)S(1)} %copy-done.2, f32[1024,768]{1,0:T(8,128)S(1)} %get-tuple-element.91.lq_ref, f32[1024,768]{1,0:T(8,128)S(1)} %get-tuple-element.92.lv_ref, ...), custom_call_target="tpu_custom_call" | custom-call | flops 8800000000 | tf_op jit(solution)/shard_map/project/pallas_call | solution.py:105
  58.1 13.0 %attend.1 = (bf16[24,512,512]{2,1,0:T(8,128)(2,1)}, bf16[1536,512]{1,0:T(8,128)(2,1)}, bf16[1024,768]{1,0:T(8,128)(2,1)S(1)}, f32[6,8,512]{2,1,0:T(8,128)}) custom-call(s32[3]{0:T(128)S(1)} %pad_add_fusion.sc_ref, bf16[1024,2304]{1,0:T(8,128)(2,1)S(1)} %get-tuple-element.96.qkv_ref.q_ref.k_ref.v_ref), custom_call_target="tpu_custom_call" | custom-call | flops 17600000000 | tf_op jit(solution)/shard_map/attend/pallas_call | solution.py:154
  73.1 1.3 collective-permute-done.17
  74.4 12.2 %feed_in.1 = (f32[1024,768]{1,0:T(8,128)S(1)}, f32[1024,128]{1,0:T(8,128)S(1)}, bf16[1024,3072]{1,0:T(8,128)(2,1)S(1)}, bf16[1024,3072]{1,0:T(8,128)(2,1)S(1)}, bf16[5,768,768]{2,1,0:T(8,128)(2,1)S(1)}) custom-call(s32[3]{0:T(128)S(1)} %pad_add_fusion.sc_ref, bf16[1024,768]{1,0:T(8,128)(2,1)S(1)} %copy-done.2, ...), custom_call_target="tpu_custom_call" | custom-call | flops 15399999488 | tf_op jit(solution)/shard_map/feed_in/pallas_call | solution.py:196
  86.7 1.7 %collective-permute-done.16 = bf16[8,192,384]{2,1,0:T(8,128)(2,1)S(1)} collective-permute-done((bf16[8,192,384]{2,1,0:T(8,128)(2,1)S(1)}, bf16[8,192,384]{2,1,0:T(8,128)(2,1)S(1)}, u32[]{:S(2)}, u32[]{:S(2)}) %collective-permute-start.16) | collective-permute-done | bytes 1179680 | tf_op jit(solution)/shard_map/ppermute | solution.py:359
  88.4 2.8 %collective-permute-done.19 = bf16[8,192,384]{2,1,0:T(8,128)(2,1)S(1)} collective-permute-done((bf16[8,192,384]{2,1,0:T(8,128)(2,1)S(1)}, bf16[8,192,384]{2,1,0:T(8,128)(2,1)S(1)}, u32[]{:S(2)}, u32[]{:S(2)}) %collective-permute-start.19) | collective-permute-done | bytes 1179680 | tf_op jit(solution)/shard_map/ppermute | solution.py:359
  91.3 21.1 %feed_out.1 = (bf16[1024,768]{1,0:T(8,128)(2,1)}, f32[1024,768]{1,0:T(8,128)S(1)}, bf16[768,1024]{1,0:T(8,128)(2,1)S(1)}, bf16[1024,3072]{1,0:T(8,128)(2,1)S(1)}) custom-call(s32[3]{0:T(128)S(1)} %pad_add_fusion.sc_ref, f32[1024,768]{1,0:T(8,128)S(1)} %get-tuple-element.104.n1_ref, ...), custom_call_target="tpu_custom_call", output_to_operand_aliasing={{3}: (3, {})} | custom-call | flops 26400000000 | tf_op jit(solution)/shard_map/feed_out/pallas_call | solution.py:239
  112.4 17.3 %attend_back.1 = (bf16[1024,2304]{1,0:T(8,128)(2,1)S(1)}, bf16[16,1024]{1,0:T(8,128)(2,1)S(1)}, f32[16,768]{1,0:T(8,128)S(1)}, f32[16,768]{1,0:T(8,128)S(1)}) custom-call(s32[3]{0:T(128)S(1)} %pad_add_fusion.sc_ref, bf16[1024,2304]{1,0:T(8,128)(2,1)} %copy-done.7, bf16[1024,2304]{1,0:T(8,128)(2,1)} %copy-done.7, bf16[1024,2304]{1,0:T(8,128)(2,1)} %copy-done.7, ...), custom_call_target="tpu_custom_call" | custom-call | flops 19800000512 | tf_op jit(solution)/shard_map/attend_back/pallas_call | solution.py:330
  131.0 1.4 collective-permute-start.23
  132.4 1.3 collective-permute-start.22
  134.6 3.4 %inputs_grad.2.rest_0_ = f32[1024,768]{1,0:T(8,128)} custom-call(f32[1024,768]{1,0:T(8,128)S(1)} %get-tuple-element.119.gfs_ref, bf16[1024,2304]{1,0:T(8,128)(2,1)S(1)} %get-tuple-element.120.d_ref, bf16[16,1024]{1,0:T(8,128)(2,1)S(1)} %get-tuple-element.121.gl, bf16[3,768,768]{2,1,0:T(8,128)(2,1)S(1)} %copy-done, bf16[16,768]{1,0:T(8,128)(2,1)S(1)} %get-tuple-element.123.dnt_ref), custom_call_target="tpu_custom_call" | custom-call | flops 3300000000 | tf_op jit(solution)/shard_map/inputs_grad/pallas_call | solution.py:349
  138.1 3.1 %collective-permute-start.26 = (f32[16,768]{1,0:T(8,128)S(1)}, f32[16,768]{1,0:T(8,128)S(1)}, u32[]{:S(2)}, u32[]{:S(2)}) collective-permute-start(f32[16,768]{1,0:T(8,128)S(1)} %add_add_fusion.1), channel_id=1, source_target_pairs={{0,24},{1,25},{2,26},{3,27},{4,28},{5,29},{6,30},{7,31},{8,16},{9,... | collective-permute-start | bytes 147464 | tf_op jit(solution)/shard_map/ppermute | solution.py:359
  141.2 1.3 collective-permute-start.24
  142.5 3.4 %inputs_grad.3 = f32[1024,768]{1,0:T(8,128)} custom-call(f32[1024,768]{1,0:T(8,128)S(1)} %get-tuple-element.119.gfs_ref, bf16[1024,2304]{1,0:T(8,128)(2,1)S(1)} %get-tuple-element.120.d_ref, bf16[16,1024]{1,0:T(8,128)(2,1)S(1)} %get-tuple-element.121.gl, bf16[3,768,768]{2,1,0:T(8,128)(2,1)S(1)} %copy-done, ...), custom_call_target="tpu_custom_call", output_to_operand_aliasing={{}: (5, {})} | custom-call | flops 3300000000 | tf_op jit(solution)/shard_map/inputs_grad/pallas_call | solution.py:349
  (129 shorter events, 13.2 us)
Async XLA Ops:
  0.6 14.8 %copy-start.10 = (bf16[24,3072]{1,0:T(8,128)(2,1)S(1)}, bf16[24,3072]{1,0:T(8,128)(2,1)}, u32[]{:S(2)}) copy-start(bf16[24,3072]{1,0:T(8,128)(2,1)} %param.23) | copy-start | bytes 442372
  3.9 14.0 %collective-permute-start.2 = (bf16[144,384]{1,0:T(8,128)(2,1)S(1)}, bf16[144,384]{1,0:T(8,128)(2,1)S(1)}, u32[]{:S(2)}, u32[]{:S(2)}) collective-permute-start(bf16[144,384]{1,0:T(8,128)(2,1)S(1)} %pad_maximum_fusion.6), channel_id=1, source_target_pairs={{0,24},{1,25},{2,26},{3,27},{4,28},{5,29},{6,30},{7,31},{8,16},{9,... | collective-permute-start | bytes 331784 | tf_op jit(solution)/shard_map/ppermute | solution.py:359
  8.9 9.6 %collective-permute-start.1 = (bf16[144,384]{1,0:T(8,128)(2,1)S(1)}, bf16[144,384]{1,0:T(8,128)(2,1)S(1)}, u32[]{:S(2)}, u32[]{:S(2)}) collective-permute-start(bf16[144,384]{1,0:T(8,128)(2,1)S(1)} %pad_maximum_fusion.6), channel_id=1, source_target_pairs={{0,16},{1,17},{2,18},{3,19},{4,20},{5,21},{6,22},{7,23},{8,24},{9,... | collective-permute-start | bytes 331784 | tf_op jit(solution)/shard_map/ppermute | solution.py:359
  8.9 9.6 %collective-permute-start = (bf16[144,384]{1,0:T(8,128)(2,1)S(1)}, bf16[144,384]{1,0:T(8,128)(2,1)S(1)}, u32[]{:S(2)}, u32[]{:S(2)}) collective-permute-start(bf16[144,384]{1,0:T(8,128)(2,1)S(1)} %pad_maximum_fusion.6), channel_id=1, source_target_pairs={{0,8},{1,9},{2,10},{3,11},{4,12},{5,13},{6,14},{7,15},{8,0},{9,1},... | collective-permute-start | bytes 331784 | tf_op jit(solution)/shard_map/ppermute | solution.py:359
  11.6 9.9 %collective-permute-start.3 = (bf16[192,384]{1,0:T(8,128)(2,1)S(1)}, bf16[192,384]{1,0:T(8,128)(2,1)S(1)}, u32[]{:S(2)}, u32[]{:S(2)}) collective-permute-start(bf16[192,384]{1,0:T(8,128)(2,1)S(1)} %bitcast.106), channel_id=1, source_target_pairs={{0,2},{1,5},{2,0},{3,7},{4,6},{5,1},{6,4},{7,3},{8,10},{9,13},{10,... | collective-permute-start | bytes 442376 | tf_op jit(solution)/shard_map/ppermute | solution.py:359
  18.5 11.1 %collective-permute-start.5 = (bf16[240,384]{1,0:T(8,128)(2,1)S(1)}, bf16[240,384]{1,0:T(8,128)(2,1)S(1)}, u32[]{:S(2)}, u32[]{:S(2)}) collective-permute-start(bf16[240,384]{1,0:T(8,128)(2,1)S(1)} %constant_dynamic-update-slice_fusion), channel_id=1, source_target_pairs={{0,16},{1,17},{2,18},{3,19},{4,20},{5,21},{6,22},{7,23},{8,24},{9,... | collective-permute-start | bytes 552968 | tf_op jit(solution)/shard_map/ppermute | solution.py:359
  20.2 9.4 %collective-permute-start.4 = (bf16[4,144,384]{2,1,0:T(8,128)(2,1)S(1)}, bf16[4,144,384]{2,1,0:T(8,128)(2,1)S(1)}, u32[]{:S(2)}, u32[]{:S(2)}) collective-permute-start(bf16[4,144,384]{2,1,0:T(8,128)(2,1)S(1)} %pad_maximum_fusion.2), channel_id=1, source_target_pairs={{0,2},{1,5},{2,0},{3,7},{4,6},{5,1},{6,4},{7,3},{8,10},{9,13},{10,... | collective-permute-start | bytes 1327112 | tf_op jit(solution)/shard_map/ppermute | solution.py:359
  21.6 13.7 %collective-permute-start.7 = (bf16[2,192,384]{2,1,0:T(8,128)(2,1)S(1)}, bf16[2,192,384]{2,1,0:T(8,128)(2,1)S(1)}, u32[]{:S(2)}, u32[]{:S(2)}) collective-permute-start(bf16[2,192,384]{2,1,0:T(8,128)(2,1)S(1)} %get-tuple-element.146), channel_id=1, source_target_pairs={{0,8},{1,9},{2,10},{3,11},{4,12},{5,13},{6,14},{7,15},{8,0},{9,1},... | collective-permute-start | bytes 884744 | tf_op jit(solution)/shard_map/ppermute | solution.py:359
  29.7 18.6 %collective-permute-start.8 = (bf16[2,240,384]{2,1,0:T(8,128)(2,1)S(1)}, bf16[2,240,384]{2,1,0:T(8,128)(2,1)S(1)}, u32[]{:S(2)}, u32[]{:S(2)}) collective-permute-start(bf16[2,240,384]{2,1,0:T(8,128)(2,1)S(1)} %pad_maximum_fusion.3), channel_id=1, source_target_pairs={{0,2},{1,5},{2,0},{3,7},{4,6},{5,1},{6,4},{7,3},{8,10},{9,13},{10,... | collective-permute-start | bytes 1105928 | tf_op jit(solution)/shard_map/ppermute | solution.py:359
  31.0 10.7 %collective-permute-start.6 = (bf16[2,240,384]{2,1,0:T(8,128)(2,1)S(1)}, bf16[2,240,384]{2,1,0:T(8,128)(2,1)S(1)}, u32[]{:S(2)}, u32[]{:S(2)}) collective-permute-start(bf16[2,240,384]{2,1,0:T(8,128)(2,1)S(1)} %pad_maximum_fusion.3), channel_id=1, source_target_pairs={{0,8},{1,9},{2,10},{3,11},{4,12},{5,13},{6,14},{7,15},{8,0},{9,1},... | collective-permute-start | bytes 1105928 | tf_op jit(solution)/shard_map/ppermute | solution.py:359
  31.8 12.3 %collective-permute-start.12 = (bf16[8,144,384]{2,1,0:T(8,128)(2,1)S(1)}, bf16[8,144,384]{2,1,0:T(8,128)(2,1)S(1)}, u32[]{:S(2)}, u32[]{:S(2)}) collective-permute-start(bf16[8,144,384]{2,1,0:T(8,128)(2,1)S(1)} %constant_dynamic-update-slice_fusion.18), channel_id=1, source_target_pairs={{0,1},{1,0},{2,3},{3,2},{4,5},{5,4},{6,7},{7,6},{8,9},{9,8},{10,11... | collective-permute-start | bytes 2654216 | tf_op jit(solution)/shard_map/ppermute | solution.py:359
  31.9 14.5 %collective-permute-start.11 = (bf16[8,144,384]{2,1,0:T(8,128)(2,1)S(1)}, bf16[8,144,384]{2,1,0:T(8,128)(2,1)S(1)}, u32[]{:S(2)}, u32[]{:S(2)}) collective-permute-start(bf16[8,144,384]{2,1,0:T(8,128)(2,1)S(1)} %constant_dynamic-update-slice_fusion.18), channel_id=1, source_target_pairs={{0,4},{1,3},{2,6},{3,1},{4,0},{5,7},{6,2},{7,5},{8,12},{9,11},{10,... | collective-permute-start | bytes 2654216 | tf_op jit(solution)/shard_map/ppermute | solution.py:359
  41.7 9.0 %collective-permute-start.9 = (bf16[2,240,384]{2,1,0:T(8,128)(2,1)S(1)}, bf16[2,240,384]{2,1,0:T(8,128)(2,1)S(1)}, u32[]{:S(2)}, u32[]{:S(2)}) collective-permute-start(bf16[2,240,384]{2,1,0:T(8,128)(2,1)S(1)} %collective-permute-done.6), channel_id=1, source_target_pairs={{0,2},{1,5},{2,0},{3,7},{4,6},{5,1},{6,4},{7,3},{8,10},{9,13},{10,... | collective-permute-start | bytes 1105928 | tf_op jit(solution)/shard_map/ppermute | solution.py:359
  42.4 28.7 %collective-permute-start.15 = (bf16[2,2,192,384]{3,2,0,1:T(8,128)(2,1)S(1)}, bf16[2,2,192,384]{3,2,0,1:T(8,128)(2,1)S(1)}, u32[]{:S(2)}, u32[]{:S(2)}) collective-permute-start(bf16[2,2,192,384]{3,2,0,1:T(8,128)(2,1)S(1)} %pad_maximum_fusion.1), channel_id=1, source_target_pairs={{0,16},{1,17},{2,18},{3,19},{4,20},{5,21},{6,22},{7,23},{8,24},{9,... | collective-permute-start | bytes 1769480 | tf_op jit(solution)/shard_map/ppermute | solution.py:359
  46.4 6.1 %collective-permute-start.13 = (bf16[8,144,384]{2,1,0:T(8,128)(2,1)S(1)}, bf16[8,144,384]{2,1,0:T(8,128)(2,1)S(1)}, u32[]{:S(2)}, u32[]{:S(2)}) collective-permute-start(bf16[8,144,384]{2,1,0:T(8,128)(2,1)S(1)} %collective-permute-done.11), channel_id=1, source_target_pairs={{0,1},{1,0},{2,3},{3,2},{4,5},{5,4},{6,7},{7,6},{8,9},{9,8},{10,11... | collective-permute-start | bytes 2654216 | tf_op jit(solution)/shard_map/ppermute | solution.py:359
  50.8 20.2 %collective-permute-start.14 = (bf16[8,240,384]{2,1,0:T(8,128)(2,1)S(1)}, bf16[8,240,384]{2,1,0:T(8,128)(2,1)S(1)}, u32[]{:S(2)}, u32[]{:S(2)}) collective-permute-start(bf16[8,240,384]{2,1,0:T(8,128)(2,1)S(1)} %constant_dynamic-update-slice_fusion.5), channel_id=1, source_target_pairs={{0,1},{1,0},{2,3},{3,2},{4,5},{5,4},{6,7},{7,6},{8,9},{9,8},{10,11... | collective-permute-start | bytes 4423688 | tf_op jit(solution)/shard_map/ppermute | solution.py:359
  50.9 20.2 %collective-permute-start.10 = (bf16[8,240,384]{2,1,0:T(8,128)(2,1)S(1)}, bf16[8,240,384]{2,1,0:T(8,128)(2,1)S(1)}, u32[]{:S(2)}, u32[]{:S(2)}) collective-permute-start(bf16[8,240,384]{2,1,0:T(8,128)(2,1)S(1)} %constant_dynamic-update-slice_fusion.5), channel_id=1, source_target_pairs={{0,4},{1,3},{2,6},{3,1},{4,0},{5,7},{6,2},{7,5},{8,12},{9,11},{10,... | collective-permute-start | bytes 4423688 | tf_op jit(solution)/shard_map/ppermute | solution.py:359
  71.1 3.3 %collective-permute-start.17 = (bf16[8,240,384]{2,1,0:T(8,128)(2,1)S(1)}, bf16[8,240,384]{2,1,0:T(8,128)(2,1)S(1)}, u32[]{:S(2)}, u32[]{:S(2)}) collective-permute-start(bf16[8,240,384]{2,1,0:T(8,128)(2,1)S(1)} %collective-permute-done.10), channel_id=1, source_target_pairs={{0,1},{1,0},{2,3},{3,2},{4,5},{5,4},{6,7},{7,6},{8,9},{9,8},{10,11... | collective-permute-start | bytes 4423688 | tf_op jit(solution)/shard_map/ppermute | solution.py:359
  71.6 15.0 %collective-permute-start.18 = (bf16[8,192,384]{2,1,0:T(8,128)(2,1)S(1)}, bf16[8,192,384]{2,1,0:T(8,128)(2,1)S(1)}, u32[]{:S(2)}, u32[]{:S(2)}) collective-permute-start(bf16[8,192,384]{2,1,0:T(8,128)(2,1)S(1)} %bitcast.68), channel_id=1, source_target_pairs={{0,1},{1,0},{2,3},{3,2},{4,5},{5,4},{6,7},{7,6},{8,9},{9,8},{10,11... | collective-permute-start | bytes 3538952 | tf_op jit(solution)/shard_map/ppermute | solution.py:359
  72.2 16.2 %collective-permute-start.16 = (bf16[8,192,384]{2,1,0:T(8,128)(2,1)S(1)}, bf16[8,192,384]{2,1,0:T(8,128)(2,1)S(1)}, u32[]{:S(2)}, u32[]{:S(2)}) collective-permute-start(bf16[8,192,384]{2,1,0:T(8,128)(2,1)S(1)} %bitcast.69), channel_id=1, source_target_pairs={{0,4},{1,3},{2,6},{3,1},{4,0},{5,7},{6,2},{7,5},{8,12},{9,11},{10,... | collective-permute-start | bytes 3538952 | tf_op jit(solution)/shard_map/ppermute | solution.py:359
  74.4 16.8 %copy-start.1 = (bf16[1024,768]{1,0:T(8,128)(2,1)S(1)}, bf16[1024,768]{1,0:T(8,128)(2,1)}, u32[]{:S(2)}) copy-start(bf16[1024,768]{1,0:T(8,128)(2,1)} %go_ref.1) | copy-start | bytes 4718596
  88.4 2.8 %collective-permute-start.19 = (bf16[8,192,384]{2,1,0:T(8,128)(2,1)S(1)}, bf16[8,192,384]{2,1,0:T(8,128)(2,1)S(1)}, u32[]{:S(2)}, u32[]{:S(2)}) collective-permute-start(bf16[8,192,384]{2,1,0:T(8,128)(2,1)S(1)} %collective-permute-done.16), channel_id=1, source_target_pairs={{0,1},{1,0},{2,3},{3,2},{4,5},{5,4},{6,7},{7,6},{8,9},{9,8},{10,11... | collective-permute-start | bytes 3538952 | tf_op jit(solution)/shard_map/ppermute | solution.py:359
  91.2 21.2 %copy-start.8 = (f32[6,8,512]{2,1,0:T(8,128)S(1)}, f32[6,8,512]{2,1,0:T(8,128)}, u32[]{:S(2)}) copy-start(f32[6,8,512]{2,1,0:T(8,128)} %get-tuple-element.114.rt_ref) | copy-start | bytes 294916
  112.4 22.2 %copy-start = (bf16[3,768,768]{2,1,0:T(8,128)(2,1)S(1)}, bf16[3,768,768]{2,1,0:T(8,128)(2,1)}, u32[]{:S(2)}) copy-start(bf16[3,768,768]{2,1,0:T(8,128)(2,1)} %get-tuple-element.122.w_ref) | copy-start | bytes 10616836
  129.7 1.3 collective-permute-start.20
  131.0 7.0 %collective-permute-start.23 = (f32[16,768]{1,0:T(8,128)S(1)}, f32[16,768]{1,0:T(8,128)S(1)}, u32[]{:S(2)}, u32[]{:S(2)}) collective-permute-start(f32[16,768]{1,0:T(8,128)S(1)} %add.63), channel_id=1, source_target_pairs={{0,6},{1,7},{2,4},{3,5},{4,2},{5,3},{6,0},{7,1},{8,14},{9,15},{10,... | collective-permute-start | bytes 147464 | tf_op jit(solution)/shard_map/ppermute | solution.py:359
  132.4 5.6 %collective-permute-start.22 = (f32[16,768]{1,0:T(8,128)S(1)}, f32[16,768]{1,0:T(8,128)S(1)}, u32[]{:S(2)}, u32[]{:S(2)}) collective-permute-start(f32[16,768]{1,0:T(8,128)S(1)} %add.63), channel_id=1, source_target_pairs={{0,4},{1,5},{2,6},{3,7},{4,0},{5,1},{6,2},{7,3},{8,12},{9,13},{10,... | collective-permute-start | bytes 147464 | tf_op jit(solution)/shard_map/ppermute | solution.py:359
  133.8 4.2 %collective-permute-start.21 = (f32[16,768]{1,0:T(8,128)S(1)}, f32[16,768]{1,0:T(8,128)S(1)}, u32[]{:S(2)}, u32[]{:S(2)}) collective-permute-start(f32[16,768]{1,0:T(8,128)S(1)} %add.63), channel_id=1, source_target_pairs={{0,2},{1,3},{2,0},{3,1},{4,6},{5,7},{6,4},{7,5},{8,10},{9,11},{10,... | collective-permute-start | bytes 147464 | tf_op jit(solution)/shard_map/ppermute | solution.py:359
  138.1 7.9 %collective-permute-start.26 = (f32[16,768]{1,0:T(8,128)S(1)}, f32[16,768]{1,0:T(8,128)S(1)}, u32[]{:S(2)}, u32[]{:S(2)}) collective-permute-start(f32[16,768]{1,0:T(8,128)S(1)} %add_add_fusion.1), channel_id=1, source_target_pairs={{0,24},{1,25},{2,26},{3,27},{4,28},{5,29},{6,30},{7,31},{8,16},{9,... | collective-permute-start | bytes 147464 | tf_op jit(solution)/shard_map/ppermute | solution.py:359
  141.2 5.0 %collective-permute-start.25 = (f32[16,768]{1,0:T(8,128)S(1)}, f32[16,768]{1,0:T(8,128)S(1)}, u32[]{:S(2)}, u32[]{:S(2)}) collective-permute-start(f32[16,768]{1,0:T(8,128)S(1)} %add_add_fusion.1), channel_id=1, source_target_pairs={{0,16},{1,17},{2,18},{3,19},{4,20},{5,21},{6,22},{7,23},{8,24},{9,... | collective-permute-start | bytes 147464 | tf_op jit(solution)/shard_map/ppermute | solution.py:359
  141.2 5.0 %collective-permute-start.24 = (f32[16,768]{1,0:T(8,128)S(1)}, f32[16,768]{1,0:T(8,128)S(1)}, u32[]{:S(2)}, u32[]{:S(2)}) collective-permute-start(f32[16,768]{1,0:T(8,128)S(1)} %add_add_fusion.1), channel_id=1, source_target_pairs={{0,8},{1,9},{2,10},{3,11},{4,12},{5,13},{6,14},{7,15},{8,0},{9,1},... | collective-permute-start | bytes 147464 | tf_op jit(solution)/shard_map/ppermute | solution.py:359
  146.2 1.3 collective-permute-start.27
  (13 other events, 165.9 us)
